TPU v7x, 32 devices: a whole 2x2x4 slice. The times are simulated.
32 devices in a mesh: dp: 8 (over z, x), section: 4 (over y, core).
Axes of the slice: x: 2, y: 2, z: 4, core: 2. Of those that a mesh axis runs over, the one named last changes fastest.
Arguments:
- tiles: bfloat16 [32, 128, 1536], P('dp'), may hold values from -6 to 6
- slide_ids: int32 [32, 128], P('dp'), may hold values from 0 to 2, never falling along the last dimension, each value on 1 to 64 neighbouring positions
- coords: int32 [2, 32, 128], P(None, 'dp'), may hold values from 0 to 255
- known: int32 [32, 3, 18], P('dp'), may hold values from 0 to 1
- labels: int32 [32, 3, 18], P('dp'), may hold values 0 or 1
- mats: float32 [4, 3, 768, 3072], P('section', None, 'dp')
- mats_m: float32 [4, 3, 768, 3072], P('section', None, 'dp'), may hold values from -5.722046e-06 to 5.722046e-06
- mats_v: float32 [4, 3, 768, 3072], P('section', None, 'dp'), may hold values from 4.455824e-12 to 1.7789412e-11
- gains: float32 [4, 2, 768], P('section')
- gains_m: float32 [4, 2, 768], P('section'), may hold values from -2.2888184e-05 to 2.2888184e-05
- gains_v: float32 [4, 2, 768], P('section'), may hold values from 7.129319e-11 to 2.846306e-10
- final_gain: float32 [768], P('section'), may hold values from 0.5 to 1.5
- fgain_m: float32 [768], P('section'), may hold values from -2.2888184e-05 to 2.2888184e-05
- fgain_v: float32 [768], P('section'), may hold values from 7.129319e-11 to 2.846306e-10
- w_in: float32 [1536, 768], P('section'), may hold values from -0.15625 to 0.15625
- win_m: float32 [1536, 768], P('section'), may hold values from -5.722046e-06 to 5.722046e-06
- win_v: float32 [1536, 768], P('section'), may hold values from 4.455824e-12 to 1.7789412e-11
- head: float32 [768, 18], P('section'), may hold values from -0.21875 to 0.21875
- head_m: float32 [768, 18], P('section'), may hold values from -5.722046e-06 to 5.722046e-06
- head_v: float32 [768, 18], P('section'), may hold values from 4.455824e-12 to 1.7789412e-11
Outputs:
- grad_norm: float32 [], replicated
- loss_sum: float32 [], replicated
- known_count: float32 [], replicated
- mats_m_new: float32 [4, 3, 768, 3072], P('section', None, 'dp')
- mats_v_new: float32 [4, 3, 768, 3072], P('section', None, 'dp')
- mats_new: float32 [4, 3, 768, 3072], P('section', None, 'dp')
- gains_m_new: float32 [4, 2, 768], P('section')
- gains_v_new: float32 [4, 2, 768], P('section')
- gains_new: float32 [4, 2, 768], P('section')
- fgain_m_new: float32 [768], P('section')
- fgain_v_new: float32 [768], P('section')
- fgain_new: float32 [768], P('section')
- win_m_new: float32 [1536, 768], P('section')
- win_v_new: float32 [1536, 768], P('section')
- win_new: float32 [1536, 768], P('section')
- head_m_new: float32 [768, 18], P('section')
- head_v_new: float32 [768, 18], P('section')
- head_new: float32 [768, 18], P('section')
Inputs may be any that keep to these rules, and one draw needn't show every extreme that they name: `slide_ids`: within a pack slide numbers never fall; each of the 3 slides has 1 to 64 tiles.
All inputs are finite; a program needn't handle non-finite values. No bound on the sum of `labels` on one device may be relied on, other than what follows from the above.
Results may differ from a plain program's by a relative error of at most 0.015.
Values may be sent and summed in bfloat16 or wider, within the bound.
No kernel may reach another device: no remote copies, remote signals or barrier semaphores. Data moves between devices by JAX's collectives and lax.ppermute only.
A program may use at most 576 MiB of HBM per device.

v0:
```python
import functools

import jax
import jax.numpy as jnp
from jax import lax
from jax.experimental import pallas as pl
from jax.experimental.pallas import tpu as pltpu
from jax.sharding import PartitionSpec as P

HEADS = 16
STEP = 10


EPS_NORM = 1e-05
CLIP = 0.05
BETA_ONE = 0.9
BETA_TWO = 0.95
ADAM_EPS = 1e-08
RATE = 0.06
RATE_GAIN = 1.0
DECAY = 0.1
RATIOS = (1, 2, 4, 8, 16)

def moved(block, route):
    dp, sections = lax.axis_size("dp"), lax.axis_size("section")
    pairs = []
    for d in range(dp):
        for s in range(sections):
            target = route(d, s)
            if target is not None:
                pairs.append((d * sections + s, target[0] * sections + target[1]))
    return lax.ppermute(block, ("dp", "section"), pairs)


def flip_dp(bit):
    return lambda d, s: (d ^ bit, s)


def flip_section(bit):
    return lambda d, s: (d, s ^ bit)


def spread_sum(value):
    dp, sections = lax.axis_size("dp"), lax.axis_size("section")
    for k in range(sections.bit_length() - 1):
        value = value + moved(value, flip_section(1 << k))
    for k in range(dp.bit_length() - 1):
        value = value + moved(value, flip_dp(1 << k))
    return value


def inner(left, right):
    return lax.dot_general(
        left, right, (((0,), (0,)), ((), ())), preferred_element_type=jnp.float32
    )


def position_table(coord, width):
    quarter = width // 4
    freq = jnp.exp(-jnp.log(10000.0) * jnp.arange(quarter, dtype=jnp.float32) / quarter)
    along = coord[0].astype(jnp.float32)[:, None] * freq
    across = coord[1].astype(jnp.float32)[:, None] * freq
    return jnp.concatenate(
        [jnp.sin(along), jnp.cos(along), jnp.sin(across), jnp.cos(across)], axis=1
    )


def log_mult(heads, tok):
    place = jnp.arange(tok, dtype=jnp.int32)
    head_idx = jnp.arange(heads, dtype=jnp.int32)
    mult = jnp.zeros((heads, tok, tok), jnp.float32)
    for ratio in RATIOS:
        hit = (place[None, :] % ratio == head_idx[:, None] % ratio).astype(jnp.float32)
        mult = mult + hit[:, :, None] * hit[:, None, :]
    return jnp.log(mult)


NN = (((1,), (0,)), ((), ()))
NT = (((1,), (1,)), ((), ()))
TN = (((0,), (0,)), ((), ()))
LANES = 128
BF = jnp.bfloat16
F32 = jnp.float32


def mm(left, right, dims=NN):
    return lax.dot_general(left, right, dims, preferred_element_type=F32)


def norm_parts(value):
    mean = jnp.mean(value, -1, keepdims=True)
    centred = value - mean
    var = jnp.mean(centred * centred, -1, keepdims=True)
    inv = lax.rsqrt(var + EPS_NORM)
    return centred * inv, inv


def norm_back(dvalue, gain, hat, inv):
    dhat = dvalue * gain
    return inv * (
        dhat
        - jnp.mean(dhat, -1, keepdims=True)
        - hat * jnp.mean(dhat * hat, -1, keepdims=True)
    )


def window(head, size):
    low = head * size // LANES * LANES
    high = -(-(head + 1) * size // LANES) * LANES
    return low, high


def placed_rows(ref, head, size):
    low, high = window(head, size)
    before, after = head * size - low, high - (head + 1) * size
    tok = ref.shape[1]
    parts = [ref[head * size : (head + 1) * size, :]]
    if before:
        parts = [jnp.zeros((before, tok), ref.dtype)] + parts
    if after:
        parts = parts + [jnp.zeros((after, tok), ref.dtype)]
    return jnp.concatenate(parts, axis=0) if len(parts) > 1 else parts[0]


def same_slide(ids_ref, pick):
    tok = ids_ref.shape[1]
    row = jnp.broadcast_to(ids_ref[pl.ds(pick, 1), :].astype(F32), (tok, tok))
    return row, row.T


def forward_kernel(
    heads, slides, shrink, scal, ids, gain, fgain, head_w, known, label,
    x0, rc, lm_v, wqkv, wo, w1, w2t, wqkv_t, wo_t, w1_t, w2, *rest
):
    fresh = rest[0]
    n_buf = 13
    rest = rest[1:] if fresh else rest[1 + n_buf :]
    send_h = rest[0]
    (x_b, qkv_b, lse_b, att_b, mid_b, gp_b, hid_b, a_b, b_b, dl_b, nl_b, dlog_b, side_b) = rest[1 : 1 + n_buf]
    (x_v, qkv_v, lse_v, att_v, mid_v, gp_v, hid_v, a_v, b_v, o_v,
     q_t, v_t, o_t, pool_v, nl_v, dlog_v, side_v, sin, sout) = rest[1 + n_buf :]
    valid, pick, first, last = scal[0], scal[1], scal[2], scal[3]
    tok, width = x_v.shape
    size = width // heads
    scale = size ** (-0.5)

    @pl.when(valid == 1)
    def _():
        @pl.when(first == 1)
        def _():
            x_v[...] = x0[pick]

        @pl.when(first != 1)
        def _():
            x_v[...] = rc[...]

        outs = []

        def emit(src, dst):
            c = pltpu.make_async_copy(src, dst, sout.at[len(outs)])
            c.start()
            outs.append(c)

        row, col = same_slide(ids, pick)
        same = row == col

        emit(x_v, x_b.at[pick])
        x = x_v[...].astype(F32)
        hat, _ = norm_parts(x)
        a_v[...] = (hat * gain[0:1, :]).astype(BF)
        emit(a_v, a_b.at[pick])
        qkv_v[...] = mm(a_v[...], wqkv[...]).astype(BF)
        emit(qkv_v, qkv_b.at[pick])
        q_t[...] = qkv_v[:, :width].T
        v_t[...] = qkv_v[:, 2 * width :].T
        for h in range(heads):
            low, high = window(h, size)
            s = mm(qkv_v[:, width + low : width + high], placed_rows(q_t, h, size)) * scale
            s = s + jnp.where(same, lm_v[h], -1000000000.0)
            top = jnp.max(s, 0, keepdims=True)
            e = jnp.exp(s - top)
            total = jnp.sum(e, 0, keepdims=True)
            lse_v[h : h + 1, :] = top + jnp.log(total)
            o = mm(v_t[h * size : (h + 1) * size, :], e.astype(BF))
            o_t[h * size : (h + 1) * size, :] = o * (1.0 / total)
        att_v[...] = o_t[...].T.astype(BF)
        emit(lse_v, lse_b.at[pick])
        emit(att_v, att_b.at[pick])
        middle = x + mm(att_v[...], wo[...])
        mid_v[...] = middle
        emit(mid_v, mid_b.at[pick])
        hat, _ = norm_parts(middle)
        b_v[...] = (hat * gain[1:2, :]).astype(BF)
        emit(b_v, b_b.at[pick])
        ff = w1.shape[1]
        part = ff // 4
        for j in range(4):
            cols = slice(j * part, (j + 1) * part)
            up = mm(b_v[...], w1[:, cols])
            square = up * up
            sig = 1.0 / (1.0 + jnp.exp(up * (-1.5957691216057308 - 0.07135481627159852 * square)))
            act = up * sig
            hid_v[:, cols] = act.astype(BF)
            slope = 1.5957691216057308 + 0.21406444881478 * square
            gp_v[:, cols] = sig + act * (1.0 - sig) * slope
        emit(gp_v, gp_b.at[pick])
        emit(hid_v, hid_b.at[pick])
        out = mid_v[...] + mm(hid_v[...], w2t[...])
        send_h[...] = out.astype(BF)

        @pl.when(last == 1)
        def _():
            o_v[...] = out
            pool_v[...] = jnp.zeros_like(pool_v)
            inverse = []
            for s in range(slides):
                inside = (col == float(s)).astype(F32)
                inverse.append(1.0 / jnp.sum(inside, 0, keepdims=True))
                parts = []
                for j in range(width // LANES):
                    parts.append(
                        jnp.sum(o_v[:, j * LANES : (j + 1) * LANES] * inside, 0, keepdims=True) * inverse[s]
                    )
                pool_v[s : s + 1, :] = jnp.concatenate(parts, axis=1)
            hat, inv = norm_parts(pool_v[...])
            low_n = (hat * fgain[...]).astype(BF)
            nl_v[...] = low_n
            logits = mm(low_n, head_w[...])
            kn = known[pick]
            lb = label[pick]
            tail = jnp.exp(-jnp.abs(logits))
            soft = jnp.maximum(logits, 0.0) + jnp.log(1.0 + tail)
            terms = kn * (soft - lb * logits)
            gate = jnp.where(logits >= 0.0, 1.0, tail) / (1.0 + tail)
            dlog = (kn * (gate - lb) * shrink).astype(BF)
            dlog_v[...] = dlog
            d_n = mm(dlog, head_w[...], NT)
            side_v[...] = jnp.zeros_like(side_v)
            side_v[0:1, :] = jnp.sum(d_n * hat, 0, keepdims=True)
            side_v[1:2, 0:LANES] = jnp.sum(terms, 0, keepdims=True)
            d_pool = norm_back(d_n, fgain[...], hat, inv)
            pool_v[...] = d_pool
            for j in range(width // LANES):
                lanes = slice(j * LANES, (j + 1) * LANES)
                acc = jnp.zeros((tok, LANES), F32)
                for s in range(slides):
                    acc = acc + jnp.where(col == float(s), pool_v[s : s + 1, lanes] * inverse[s], 0.0)
                o_v[:, lanes] = acc
            tails = [
                pltpu.make_async_copy(o_v, dl_b.at[pick], sin.at[0]),
                pltpu.make_async_copy(nl_v, nl_b.at[pick], sin.at[1]),
                pltpu.make_async_copy(dlog_v, dlog_b.at[pick], sin.at[2]),
                pltpu.make_async_copy(side_v, side_b.at[pick], sin.at[3]),
            ]
            for c in tails:
                c.start()
            for c in tails:
                c.wait()

        for c in outs:
            c.wait()


def backward_kernel(
    heads, scal, ids, gain, rc_v, dl_b, lm_v, wqkv_t, wo_t, w1_t, w2,
    x_b, qkv_b, lse_b, mid_b, gp_b, *rest
):
    fresh = rest[0]
    n_buf = 5
    rest = rest[1:] if fresh else rest[1 + n_buf :]
    send_h = rest[0]
    outs = rest[1 : 1 + n_buf]
    (dl_v, x_v, qkv_v, lse_v, mid_v, gp_v, dm_v, q_t, k_t, do_v, do_t, dq_t, p_v, ds_v, sin) = rest[1 + n_buf :]
    valid, pick, last = scal[0], scal[1], scal[3]
    dbr_v, dup_v, dat_v, dqkv_v, gg_v = [ref.at[pick] for ref in outs]
    tok, width = x_v.shape
    size = width // heads
    scale = size ** (-0.5)
    per = 8

    @pl.when(valid == 1)
    def _():
        from_head = pltpu.make_async_copy(dl_b.at[pick], dl_v, sin.at[0])

        @pl.when(last == 1)
        def _():
            from_head.start()

        loads = [
            pltpu.make_async_copy(gp_b.at[pick], gp_v, sin.at[1]),
            pltpu.make_async_copy(mid_b.at[pick], mid_v, sin.at[2]),
            pltpu.make_async_copy(qkv_b.at[pick], qkv_v, sin.at[3]),
            pltpu.make_async_copy(lse_b.at[pick], lse_v, sin.at[4]),
            pltpu.make_async_copy(x_b.at[pick], x_v, sin.at[5]),
        ]
        for c in loads:
            c.start()
        row, col = same_slide(ids, pick)
        same = row == col

        @pl.when(last == 1)
        def _():
            from_head.wait()

        @pl.when(last != 1)
        def _():
            dl_v[...] = rc_v[...].astype(F32)

        dbr_v[...] = dl_v[...].astype(BF)
        loads[0].wait()
        ff = w2.shape[1]
        part = ff // 4
        for j in range(4):
            cols = slice(j * part, (j + 1) * part)
            dup_v[:, cols] = (mm(dbr_v[...], w2[:, cols]) * gp_v[:, cols]).astype(BF)
        d_b = mm(dup_v[...], w1_t[...])
        loads[1].wait()
        hat, inv = norm_parts(mid_v[...])
        gg_v[1:2, :] = jnp.sum(d_b * hat, 0, keepdims=True)
        d_mid = dl_v[...] + norm_back(d_b, gain[1:2, :], hat, inv)
        dm_v[...] = d_mid
        dat_v[...] = d_mid.astype(BF)
        loads[2].wait()
        q_t[...] = qkv_v[:, :width].T
        k_t[...] = qkv_v[:, width : 2 * width].T
        do_v[...] = mm(dat_v[...], wo_t[...]).astype(BF)
        do_t[...] = do_v[...].T
        loads[3].wait()
        lane = lax.broadcasted_iota(jnp.int32, (tok, LANES), 1)
        for group in range(heads // per):
            for i in range(per):
                h = group * per + i
                low, high = window(h, size)
                s = mm(qkv_v[:, width + low : width + high], placed_rows(q_t, h, size)) * scale
                s = s + jnp.where(same, lm_v[h], -1000000000.0)
                p = jnp.exp(s - lse_v[h : h + 1, :])
                dp = mm(qkv_v[:, 2 * width + low : 2 * width + high], placed_rows(do_t, h, size))
                inner_sum = jnp.sum(dp * p, 0, keepdims=True)
                ds = (p * (dp - inner_sum)).astype(BF)
                p_v[:, i * tok : (i + 1) * tok] = p.astype(BF)
                ds_v[:, i * tok : (i + 1) * tok] = ds
                dq_t[h * size : (h + 1) * size, :] = mm(k_t[h * size : (h + 1) * size, :], ds) * scale
            base = group * per * size
            for block in range(base // LANES, (base + per * size) // LANES):
                left = block * LANES
                inside = [
                    i for i in range(per)
                    if (group * per + i) * size < left + LANES and (group * per + i + 1) * size > left
                ]
                spans = slice(inside[0] * tok, (inside[-1] + 1) * tok)
                q_parts, o_parts = [], []
                for i in inside:
                    start = (group * per + i) * size - left
                    keep = (lane >= start) & (lane < start + size)
                    q_parts.append(jnp.where(keep, qkv_v[:, left : left + LANES], jnp.zeros((), BF)))
                    o_parts.append(jnp.where(keep, do_v[:, left : left + LANES], jnp.zeros((), BF)))
                dk = mm(ds_v[:, spans], jnp.concatenate(q_parts, axis=0)) * scale
                dv = mm(p_v[:, spans], jnp.concatenate(o_parts, axis=0))
                dqkv_v[:, width + left : width + left + LANES] = dk.astype(BF)
                dqkv_v[:, 2 * width + left : 2 * width + left + LANES] = dv.astype(BF)
        dqkv_v[:, :width] = dq_t[...].T.astype(BF)
        d_a = mm(dqkv_v[...], wqkv_t[...])
        loads[4].wait()
        hat, inv = norm_parts(x_v[...].astype(F32))
        gg_v[0:1, :] = jnp.sum(d_a * hat, 0, keepdims=True)
        send_h[...] = (dm_v[...] + norm_back(d_a, gain[0:1, :], hat, inv)).astype(BF)


def spec_any():
    return pl.BlockSpec(memory_space=pltpu.HBM)


def spec_vmem():
    return pl.BlockSpec(memory_space=pltpu.VMEM)


def resident(value):
    return pltpu.with_memory_space_constraint(value, pltpu.VMEM)


def in_hbm(value):
    return pltpu.with_memory_space_constraint(value, pltpu.HBM)


def after(value, *others):
    return lax.optimization_barrier((value, *others))[0]


def load_body(cuts, plans, scal, *refs):
    n_out = sum(len(c) for c in cuts)
    n_in = len(refs) - 2 * n_out - 1
    pieces, straight, turned, sems = (
        refs[:n_in], refs[n_in : n_in + n_out], refs[n_in + n_out : -1], refs[-1]
    )

    def copies_of(chunk, flag):
        base = sum(len(c) for c in cuts[:chunk])
        out = []
        for n, (piece, place, part) in enumerate(plans[flag]):
            src = pieces[piece] if part is None else pieces[piece].at[part]
            src = src.at[chunk]
            rows = pl.ds(pl.multiple_of(scal[1 + place], 16), src.shape[0])
            for j, (low, high) in enumerate(cuts[chunk]):
                out.append(
                    pltpu.make_async_copy(
                        src.at[:, low:high], straight[base + j].at[rows, :], sems.at[chunk, n, j]
                    )
                )
        return out

    for flag in range(2):

        @pl.when(scal[0] == flag)
        def _():
            for chunk in range(len(cuts)):
                for copy in copies_of(chunk, flag):
                    copy.start()

    base = 0
    for chunk, cut in enumerate(cuts):
        for flag in range(2):

            @pl.when(scal[0] == flag)
            def _():
                for copy in copies_of(chunk, flag):
                    copy.wait()

        for j in range(base, base + len(cut)):
            step = 256

            def turn(index, carry):
                here = pl.ds(pl.multiple_of(index * step, step), step)
                turned[j][:, here] = straight[j][here, :].T
                return carry

            lax.fori_loop(0, straight[j].shape[0] // step, turn, 0)
        base += len(cut)


def load_weights(pieces, plans, scal, cuts, rows):
    sizes = [high - low for cut in cuts for low, high in cut]
    most = max(len(plan) for plan in plans)
    return pl.pallas_call(
        functools.partial(load_body, cuts, plans),
        out_shape=[pltpu.VMEM((rows, n), BF) for n in sizes] + [pltpu.VMEM((n, rows), BF) for n in sizes],
        in_specs=[pl.BlockSpec(memory_space=pltpu.SMEM)]
        + [pl.BlockSpec(memory_space=pl.ANY)] * len(pieces),
        out_specs=[spec_vmem()] * (2 * len(sizes)),
        scratch_shapes=[pltpu.SemaphoreType.DMA((len(cuts), most, 2))],
        compiler_params=pltpu.CompilerParams(vmem_limit_bytes=8 << 20),
        name="load_weights",
    )(scal, *[in_hbm(piece) for piece in pieces])


def weight_grads_body(shape, order, *refs):
    rows, micro, tok = shape
    lefts, rights, outs = refs[:4], refs[4:8], refs[8:11]
    turned, ordered, grad, left_v, hid_v, sin, sout = refs[11:]
    loads = [pltpu.make_async_copy(lefts[n], left_v.at[n], sin.at[n]) for n in range(3)]
    wide = pltpu.make_async_copy(rights[3], hid_v, sin.at[3])
    for copy in loads:
        copy.start()
    wide.start()
    taken = ordered.shape[0]
    cuts = (slice(0, rows), slice(rows, taken // 2), slice(taken // 2, taken))
    step = 768
    copies = []
    attn_cols = rights[1].shape[2]
    for chunk, n, col in ((1, 0, 0), (0, 1, 0), (0, 2, attn_cols), (2, 3, 0)):
        if n < 3:
            loads[n].wait()
            left, right = left_v.at[n], rights[n]
        else:
            wide.wait()
            left, right = lefts[3], hid_v
        for p in range(micro):
            turned[:, p * tok : (p + 1) * tok] = left[p].T
        for k in range(taken // rows):
            here = pl.ds(pl.multiple_of(order[k] * rows, 16), rows)
            ordered[k * rows : (k + 1) * rows, :] = turned[here, :]
        for start in range(0, right.shape[2], step):
            block = right[:, :, start : start + step].reshape(micro * tok, step)
            for low in range(0, taken, taken // 2):
                grad[chunk, low : low + taken // 2, col + start : col + start + step] = mm(
                    ordered[low : low + taken // 2, :], block
                ).astype(BF)
        if n == 1:
            continue
        for m, cut in enumerate(cuts):
            copy = pltpu.make_async_copy(grad.at[chunk, cut], outs[m].at[chunk], sout.at[chunk, m])
            copy.start()
            copies.append(copy)
    for copy in copies:
        copy.wait()


def weight_grads(order, lefts, rights, rows):
    micro, tok, width = lefts[0].shape
    cols = rights[0].shape[2]
    taken = order.shape[0] * rows
    return pl.pallas_call(
        functools.partial(weight_grads_body, (rows, micro, tok)),
        out_shape=[pltpu.HBM((3, n, cols), BF) for n in (rows, taken // 2 - rows, taken // 2)],
        in_specs=[pl.BlockSpec(memory_space=pltpu.SMEM)]
        + [spec_any()] * 3 + [spec_vmem()] * 4 + [spec_any()],
        out_specs=[spec_any()] * 3,
        scratch_shapes=[
            pltpu.VMEM((width, micro * tok), BF), pltpu.VMEM((taken, micro * tok), BF),
            pltpu.VMEM((3, taken, cols), BF), pltpu.VMEM((3, micro, tok, width), BF),
            pltpu.VMEM((micro, tok, cols), BF),
            pltpu.SemaphoreType.DMA((4,)), pltpu.SemaphoreType.DMA((3, 3)),
        ],
        compiler_params=pltpu.CompilerParams(vmem_limit_bytes=34 << 20),
        cost_estimate=pl.CostEstimate(
            flops=6 * micro * tok * taken * cols, bytes_accessed=12 * taken * cols, transcendentals=0
        ),
        name="weight_grads",
    )(
        order, *[in_hbm(v) for v in lefts[:3]], resident(lefts[3]),
        *[resident(v) for v in rights[:3]], in_hbm(rights[3]),
    )


def forward_call(heads, slides, shrink, scal, ids, gain, fgain, head_w, known, label, x0, received, lm, weights, bufs):
    micro, tok, width = x0.shape
    ff = weights[2].shape[1]
    rows = known.shape[1]
    shapes = [
        ((tok, width), BF), ((tok, 3 * width), BF), ((heads, tok), F32), ((tok, width), BF),
        ((tok, width), F32), ((tok, ff), F32), ((tok, ff), BF), ((tok, width), BF), ((tok, width), BF),
        ((tok, width), F32), ((rows, width), BF), ((rows, LANES), BF), ((8, width), F32),
    ]
    fresh = bufs is None
    given = [] if fresh else list(bufs)
    vm = lambda index: pltpu.VMEM(*shapes[index])
    n_in = 18
    out = pl.pallas_call(
        functools.partial(forward_body, heads, slides, shrink, fresh),
        out_shape=[pltpu.VMEM((tok, width), BF)]
        + [pltpu.HBM((micro,) + s, d) for s, d in shapes],
        in_specs=[pl.BlockSpec(memory_space=pltpu.SMEM)]
        + [spec_vmem()] * 17
        + [spec_any()] * len(given),
        out_specs=[spec_vmem()] + [spec_any()] * len(shapes),
        input_output_aliases={n_in + i: 1 + i for i in range(len(given))},
        scratch_shapes=[
            vm(0), vm(1), vm(2), vm(3), vm(4), vm(5), vm(6), vm(7), vm(8),
            pltpu.VMEM((tok, width), F32),
            pltpu.VMEM((width, tok), BF), pltpu.VMEM((width, tok), BF), pltpu.VMEM((width, tok), F32),
            pltpu.VMEM((rows, width), F32), vm(10), vm(11), vm(12),
            pltpu.SemaphoreType.DMA((4,)), pltpu.SemaphoreType.DMA((9,)),
        ],
        compiler_params=pltpu.CompilerParams(vmem_limit_bytes=14 << 20),
        cost_estimate=pl.CostEstimate(flops=7 << 30, bytes_accessed=8 << 20, transcendentals=1 << 20),
        name="layer_forward",
    )(
        scal, ids, gain, fgain, head_w, known, label, resident(x0), received, resident(lm),
        *[resident(w) for w in weights], *[in_hbm(b) for b in given],
    )
    return out[0], out[1:]


def backward_call(heads, scal, ids, gain, received, records, lm, weights, bufs):
    x_b, qkv_b, lse_b, mid_b, gp_b, dl_b = records
    micro, tok, width = x_b.shape
    ff = weights[3].shape[1]
    shapes = [((tok, width), BF), ((tok, ff), BF), ((tok, width), BF), ((tok, 3 * width), BF), ((8, width), F32)]
    fresh = bufs is None
    given = [] if fresh else list(bufs)
    n_in = 15
    out = pl.pallas_call(
        functools.partial(backward_body, heads, fresh),
        out_shape=[pltpu.VMEM((tok, width), BF)]
        + [pltpu.VMEM((micro,) + s, d) for s, d in shapes],
        in_specs=[pl.BlockSpec(memory_space=pltpu.SMEM)] + [spec_vmem()] * 3 + [spec_any()]
        + [spec_vmem()] * 5 + [spec_any()] * 5 + [spec_vmem()] * len(given),
        out_specs=[spec_vmem()] * (1 + len(shapes)),
        input_output_aliases={n_in + i: 1 + i for i in range(len(given))},
        scratch_shapes=[
            pltpu.VMEM((tok, width), F32),
            pltpu.VMEM((tok, width), BF), pltpu.VMEM((tok, 3 * width), BF), pltpu.VMEM((heads, tok), F32),
            pltpu.VMEM((tok, width), F32), pltpu.VMEM((tok, ff), F32),
        ]
        + [
            pltpu.VMEM((tok, width), F32),
            pltpu.VMEM((width, tok), BF), pltpu.VMEM((width, tok), BF),
            pltpu.VMEM((tok, width), BF), pltpu.VMEM((width, tok), BF), pltpu.VMEM((width, tok), F32),
            pltpu.VMEM((tok, 8 * tok), BF), pltpu.VMEM((tok, 8 * tok), BF),
            pltpu.SemaphoreType.DMA((6,)),
        ],
        compiler_params=pltpu.CompilerParams(vmem_limit_bytes=14 << 20),
        cost_estimate=pl.CostEstimate(flops=10 << 30, bytes_accessed=8 << 20, transcendentals=1 << 20),
        name="layer_backward",
    )(
        scal, ids, gain, received, in_hbm(dl_b), resident(lm), *[resident(w) for w in weights],
        *[in_hbm(b) for b in (x_b, qkv_b, lse_b, mid_b, gp_b)], *[resident(b) for b in given],
    )
    return out[0], out[1:]


def forward_body(heads, slides, shrink, fresh, *refs):
    forward_kernel(heads, slides, shrink, *refs[:18], fresh, *refs[18:])


def backward_body(heads, fresh, *refs):
    backward_kernel(heads, *refs[:15], fresh, *refs[15:])


def adam(weight, grad, first, second, rate, decay):
    first = BETA_ONE * first + (1.0 - BETA_ONE) * grad
    second = BETA_TWO * second + (1.0 - BETA_TWO) * grad * grad
    mhat = first / (1.0 - BETA_ONE**STEP)
    vhat = second / (1.0 - BETA_TWO**STEP)
    return (first, second, weight - rate * (mhat / (jnp.sqrt(vhat) + ADAM_EPS) + decay * weight))


def per_device(
    tiles,
    slide_ids,
    coords,
    known,
    labels,
    mats,
    mats_m,
    mats_v,
    gains,
    gains_m,
    gains_v,
    final_gain,
    fgain_m,
    fgain_v,
    w_in,
    win_m,
    win_v,
    head,
    head_m,
    head_v,
):
    sections = lax.axis_size("section")
    dp = lax.axis_size("dp")
    section = lax.axis_index("section")
    dp_index = lax.axis_index("dp")
    near = dp // 2
    side_of, place = dp_index // near, dp_index % near
    row_of, core = section // 2, section % 2
    stage = 2 * row_of + (side_of ^ row_of)
    micro, tok = slide_ids.shape
    heads = HEADS
    slides, genes = known.shape[1:]
    width = w_in.shape[1]
    rows, wide_cols = mats.shape[2:]
    direct = dp == 8 and sections == 4 and rows % 32 == 0

    def join(side, place, row, core):
        return side * near + place, row * 2 + core

    def layer_turn(d, s):
        side, at, row, c = d // near, d % near, s // 2, s % 2
        target = join(c ^ row, at, row, side ^ row)
        return None if target == (d, s) else target

    def pack_turn(d, s):
        side, at, row, c = d // near, d % near, s // 2, s % 2
        target = join(c, at, row, side)
        return None if target == (d, s) else target

    own_layer = side_of == (core ^ row_of)
    own_packs = side_of == core

    def slot(flip_c, flip_m):
        return (core ^ flip_c ^ row_of) * near + (place ^ flip_m)

    groups = [
        [
            (side * near + m) * sections + row * 2 + (half ^ row)
            for half in range(2)
            for m in range(near)
        ]
        for side in range(2)
        for row in range(sections // 2)
    ]

    def to_next(distance):
        def route(d, s):
            side, at, row, c = d // near, d % near, s // 2, s % 2
            goal = 2 * row + (side ^ row) + distance
            if not 0 <= goal < sections:
                return None
            return join((goal % 2) ^ (goal // 2), at, goal // 2, c)

        return route

    def some(route, kind):
        def limited(d, s):
            own = d // near == ((s % 2) ^ (s // 2))
            target = route(d, s)
            return target if kind is None or own == kind else None

        return limited

    def gather_all(low, early, late):
        if not direct:
            own = jnp.where(own_layer, low, moved(low, layer_turn))
            full = lax.all_gather(
                own, ("dp", "section"), axis=1, tiled=True, axis_index_groups=groups
            )
            table = early(())
            marks = late(table[0])
            return [full], ([(0, 0, None)], [(0, 0, None)]), jnp.zeros((2,), jnp.int32), table, marks
        half = rows // 2

        def routes(kind):
            return [some(f, kind) for f in (flip_dp(1), flip_dp(2), flip_section(1))]

        x_own, z_own, c_own = routes(True)
        x_got, z_got, c_got = routes(False)
        together = lax.optimization_barrier
        low = low.reshape(3, 2, half, wide_cols).transpose(1, 0, 2, 3)
        got, side, over = together(
            (moved(low, layer_turn), moved(low, x_own), moved(low, z_own))
        )
        table = early(())
        marks = late(got)
        side_got, over_got, far_low, far_high, sent, sent_got, table = together(
            (
                moved(got, x_got), moved(got, z_got), moved(over[0], x_own), moved(side[1], z_own),
                moved(low, c_own), moved(got, c_got), table,
            )
        )
        far_low_got, far_high_got, sent_side, sent_over, sent_low, sent_high, sent_side_got, sent_over_got = together(
            (
                moved(over_got[0], x_got), moved(side_got[1], z_got),
                moved(side, c_own), moved(over, c_own),
                moved(far_low, c_own), moved(far_high, c_own),
                moved(side_got, c_got), moved(over_got, c_got),
            )
        )
        mine_own = [low, side, over, far_low, far_high]
        sent_own = [sent, sent_side, sent_over, sent_low, sent_high]
        mine_got = [got, side_got, over_got, far_low_got, far_high_got]
        sent_got = [
            sent_got, sent_side_got, sent_over_got, moved(far_low_got, c_got), moved(far_high_got, c_got),
        ]
        pieces = mine_own + sent_own + mine_got + sent_got
        def listed(first, place):
            out = []
            for n in range(3):
                out += [(first + n, place + 2 * n + h, h) for h in range(2)]
            return out + [(first + 3 + h, place + 6 + h, None) for h in range(2)]

        plans = (listed(10, 0) + listed(5, 8), listed(0, 0) + listed(15, 8))
        starts = [
            slot(flip_c, m) * rows + start
            for flip_c in range(2)
            for m in range(4)
            for start in (0, half)
        ]
        place_at = jnp.stack([own_layer.astype(jnp.int32)] + starts).astype(jnp.int32)
        return pieces, plans, place_at, table, marks

    def scatter_all(lefts, rights):
        order = jnp.stack([slot(1 - k // 4, (k + 3) % 4) for k in range(8)]).astype(jnp.int32)
        if not direct:
            flat = lambda v: v.reshape((-1, v.shape[-1]))
            grads = [inner(flat(l), flat(r)).astype(BF) for l, r in zip(lefts, rights)]
            outs = []
            for grad in (grads[0], jnp.concatenate(grads[1:3], axis=1), grads[3]):
                own = lax.psum_scatter(
                    grad, ("dp", "section"), scatter_dimension=0, tiled=True, axis_index_groups=groups
                )
                outs.append((own, jnp.where(own_layer, own, moved(own, layer_turn)).astype(F32)))
            squares = sum(jnp.sum(jnp.square(own.astype(F32))) for own, _ in outs)
            mark = outs[0][0]
            held = beside_z(beside_x(beside_early(mark), mark), mark)
            return jnp.stack([outs[n][1] for n in (1, 0, 2)]), settled(*beside_last(held, mark), squares)
        half = rows // 2
        send_far, send_rest, kept = weight_grads(order, lefts, rights, rows)
        got_far = moved(send_far, flip_section(1))
        got_rest = moved(after(send_rest, got_far), flip_section(1))
        kept = kept.reshape(3, 4, rows, wide_cols)
        got_rest = got_rest.reshape(3, 3, rows, wide_cols)

        def both(m, cut=slice(None)):
            other = got_far[:, cut] if m == 0 else got_rest[:, m - 1, cut]
            return kept[:, m, cut].astype(F32) + other.astype(F32)

        far_low, far_high = lax.optimization_barrier(
            (both(0, slice(0, half)).astype(BF), both(0, slice(half, rows)).astype(BF))
        )
        first = beside_early(far_low)
        from_side, from_over = moved(far_low, flip_dp(1)), moved(far_high, flip_dp(2))
        from_side, from_over = lax.optimization_barrier((from_side, from_over))
        low_rows = ((0, 0), (0, rows - half), (0, 0))
        high_rows = ((0, 0), (half, 0), (0, 0))
        side = both(2) + jnp.pad(from_over, high_rows).astype(F32)
        over = both(3) + jnp.pad(from_side, low_rows).astype(F32)
        side, over = lax.optimization_barrier((side.astype(BF), over.astype(BF)))

        def totalled(kind, mark):
            one, two = lax.optimization_barrier(
                (moved(side, some(flip_dp(1), kind)), moved(over, some(flip_dp(2), kind)), mark)
            )[:2]
            return after((both(1) + one.astype(F32) + two.astype(F32)).astype(BF))

        second = beside_x(first, side)
        third = beside_z(second, side)
        total_far = totalled(False, third)
        away = moved(total_far, layer_turn)
        side, over = lax.optimization_barrier((side, over, total_far))[:2]
        total_own = totalled(True, ())
        small, piece = beside_last(third, total_own)
        squares = jnp.where(
            own_layer,
            jnp.sum(jnp.square(total_own.astype(F32))),
            jnp.sum(jnp.square(total_far.astype(F32))),
        )
        ends = settled(small, piece, squares)
        away, ends = lax.optimization_barrier((away, ends))
        return jnp.where(own_layer, total_own, away).astype(F32), ends

    def over_section(block):
        other_row = moved(block, flip_section(3))
        pair = jnp.stack([block, other_row])
        other_core = moved(pair, flip_section(1))
        whole = jnp.zeros((sections,) + block.shape, block.dtype)
        for part, flip in ((block, 0), (other_row, 3), (other_core[0], 1), (other_core[1], 2)):
            whole = lax.dynamic_update_slice(
                whole, part[None], (section ^ flip,) + (0,) * block.ndim
            )
        return whole.reshape((sections * block.shape[0],) + block.shape[1:])

    slots = micro * dp * slides * genes
    shrink = 0.5 ** (slots - 1).bit_length()
    def to_first(d, s):
        return (d - near, s) if d >= near and s < 2 else None

    def to_home(d, s):
        return (d + near, s) if d < near and s < 2 else None

    in_rows = w_in.shape[0]

    def embedded(mark):
        own_part, in_rows = final_gain.shape[0], w_in.shape[0]
        gain_high = final_gain.astype(BF)
        gain_low = (final_gain - gain_high.astype(F32)).astype(BF)
        own_ends = jnp.concatenate([head.astype(BF), gain_high[:, None], gain_low[:, None]], axis=1)
        own_ends = jnp.pad(own_ends, ((0, 0), (0, LANES - genes - 2)))
        extra = own_part * LANES // width
        packed = over_section(
            after(jnp.concatenate([w_in.astype(BF), own_ends.reshape(extra, width)])[None], mark)
        )
        in_low = packed[:, :in_rows].reshape(sections * in_rows, width)
        head_p = packed[:, in_rows:].reshape(sections * own_part, LANES)
        full_fgain = (head_p[:, genes].astype(F32) + head_p[:, genes + 1].astype(F32))[None, :]
        table = jax.vmap(lambda c: position_table(c, width), in_axes=1)(after(coords, mark))
        x0 = (
            jnp.dot(tiles.reshape(micro * tok, -1), in_low, preferred_element_type=F32).reshape(
                micro, tok, width
            )
            + table
        ).astype(BF)

        return x0, head_p, full_fgain

    cuts = (((0, 3 * width), (3 * width, wide_cols)), ((0, wide_cols),), ((0, wide_cols),))
    half_packs = micro // 2

    def mine_of(value):
        return lax.dynamic_slice_in_dim(value, core * half_packs, half_packs, 0)

    def exchanged(x0):
        first, known_in, labels_in = lax.optimization_barrier((slide_ids, known, labels, x0))[:3]
        home = mine_of(
            jnp.concatenate(
                [first, known_in.reshape(micro, -1), labels_in.reshape(micro, -1)], axis=1
            )
        )
        other = moved(home, flip_dp(near))
        lower = side_of == 0
        home = jnp.concatenate([jnp.where(lower, home, other), jnp.where(lower, other, home)])
        gain = jnp.where(own_layer, gains[0], moved(gains[0], flip_section(1)))
        return home, gain

    pieces, plans, place_at, (x0, head_p, full_fgain), (home, gain) = gather_all(
        mats[0].astype(BF), embedded, exchanged
    )
    near_packs = mine_of(x0)
    far_packs = moved(near_packs, to_first)
    x0_near = jnp.concatenate([near_packs, near_packs])
    ids = home[:, :tok]
    marks = home[:, tok:].reshape(micro, 2, slides, genes).astype(F32)
    pad = ((0, 0), (0, 16 - slides), (0, LANES - genes))
    known_p = jnp.pad(marks[:, 0], pad)
    labels_p = jnp.pad(marks[:, 1], pad)
    x0_near, lm, ids, gain, pieces, full_fgain, head_p, known_p, labels_p = lax.optimization_barrier(
        (x0_near, log_mult(heads, tok), ids, gain, pieces, full_fgain, head_p, known_p, labels_p)
    )
    wqkv, wo, w1, w2, wqkv_t, wo_t, w1_t, w2_t = load_weights(pieces, plans, place_at, cuts, width)
    ticks = micro + 2 * (sections - 1)
    late = 2 * (sections - 1)
    def scalars(index):
        valid = (index >= 0) & (index < micro)
        return jnp.stack(
            [valid, jnp.clip(index, 0, micro - 1), stage == 0, stage == sections - 1]
        ).astype(jnp.int32)

    arrived = [jnp.zeros((tok, width), BF)] * 2
    bufs = None
    for tick in range(ticks):
        if tick == half_packs:
            x0_near = jnp.concatenate([near_packs, after(far_packs, send)])
        end_args = (full_fgain, head_p, known_p, labels_p)
        send, bufs = forward_call(
            heads, slides, shrink, scalars(tick - 2 * stage), ids, gain, *end_args, x0_near, arrived[tick], lm,
            (wqkv, wo, w1, w2_t, wqkv_t, wo_t, w1_t, w2), bufs,
        )
        arrived.append(moved(send, to_next(1)) if tick + 2 < ticks else None)
    (x_b, qkv_b, lse_b, att_b, mid_b, gp_b, hid_b, a_b, b_b, dl_b, nl_b, dlog_b, side_b) = bufs
    records = (x_b, qkv_b, lse_b, mid_b, gp_b, dl_b)
    arrived = [jnp.zeros((tok, width), BF)] * 2
    bufs = None
    sends = []
    for tick in range(ticks):
        send, bufs = backward_call(
            heads, scalars(tick - 2 * (sections - 1 - stage)), ids, gain, arrived[tick], records,
            lm, (wqkv_t, wo_t, w1_t, w2), bufs,
        )
        sends.append(send)
        arrived.append(moved(send, to_next(-1)) if tick + 2 < ticks else None)
    dbr_b, dup_b, dat_b, dqkv_b, gg_b = bufs
    nl_b, dlog_b, side_b = lax.optimization_barrier((nl_b, dlog_b, side_b, sends[-1]))[:3]
    flat = lambda v: v.reshape((-1, v.shape[-1]))
    bits = [1 << k for k in range(dp.bit_length() - 1)]
    on_last = stage == sections - 1

    def halved(piece, bit):
        size = piece.shape[0] // 2
        up = (dp_index // bit) % 2
        keep = lax.dynamic_slice_in_dim(piece, up * size, size, 0)
        away = lax.dynamic_slice_in_dim(piece, (1 - up) * size, size, 0)
        return (keep.astype(F32) + moved(away, flip_dp(bit)).astype(F32)).astype(BF)

    d_near = jnp.stack(sends[late : late + half_packs])
    d_far = jnp.stack([moved(send, to_home) for send in sends[late + half_packs :]])
    d_rows = jnp.where(stage == 0, d_near, jnp.where(row_of == 0, d_far, jnp.zeros((), BF)))

    def beside_early(mark):
        rows_in = after(d_rows, mark)
        rows_in = rows_in + moved(rows_in, lambda d, s: (d, s ^ 2) if s < 2 else None)
        other = moved(rows_in, flip_section(1))
        rows_in = jnp.concatenate(
            [jnp.where(core == 0, rows_in, other), jnp.where(core == 0, other, rows_in)]
        )
        mine = lax.dynamic_slice_in_dim(flat(tiles), section * in_rows, in_rows, 1)
        piece = inner(mine, flat(rows_in)).astype(BF)
        grad_head = jnp.where(on_last, inner(flat(nl_b), flat(dlog_b)), 0.0)[:, :genes]
        side = jnp.where(on_last, jnp.sum(side_b, 0), 0.0)
        seen = jnp.pad(jnp.sum(marks[:, 0]).reshape(1), (0, LANES - 1))
        small = jnp.concatenate(
            [jnp.sum(gg_b, 0)[:2].reshape(-1), seen, side[0], grad_head.reshape(-1), side[1, :LANES]]
        )
        return small + moved(small, flip_section(1)), piece

    def folded(held, bit, mark):
        small, piece = lax.optimization_barrier((*held, mark))[:2]
        return small + moved(small, flip_dp(bit)), halved(piece, bit)

    def beside_x(held, mark):
        return folded(held, bits[0], mark)

    def beside_z(held, mark):
        for bit in bits[1:-1]:
            held = folded(held, bit, mark)
        return held

    def beside_last(held, mark):
        small, piece = lax.optimization_barrier((*held, mark))[:2]
        return small, (piece.astype(F32) + moved(piece, flip_dp(bits[-1])).astype(F32)).astype(BF)

    n_gain = 2 * width
    lead = (place == 0) & (core == 0)

    def settled(small, piece, squares):
        layer_gain, ends = small[:n_gain].reshape(2, width), small[n_gain + LANES :]
        count = jnp.maximum(small[n_gain], 1.0)
        own_ends = jnp.where(on_last, ends, 0.0)
        squares = (
            squares
            + 0.5 * jnp.sum(jnp.square(piece.astype(F32)))
            + jnp.where(lead, jnp.sum(layer_gain * layer_gain), 0.0)
            + jnp.where(lead, jnp.sum(own_ends[: width + width * genes] ** 2), 0.0)
        )
        sum_gain = jnp.where(own_layer, layer_gain, moved(layer_gain, flip_dp(near)))
        ends = own_ends + moved(own_ends, flip_section(2))
        ends = ends + moved(ends, flip_dp(near))
        sum_fgain = ends[:width]
        sum_head = ends[width : width + width * genes].reshape(width, genes)
        loss_sum = jnp.sum(ends[width + width * genes :])
        part = width // sections
        part_head = lax.dynamic_slice_in_dim(sum_head, section * part, part, 0)
        part_fgain = lax.dynamic_slice_in_dim(sum_fgain, section * part, part, 0)
        return squares.reshape(1, 1), piece, count, loss_sum, sum_gain, part_head, part_fgain

    shards, (squares, piece, count, loss_sum, sum_gain, part_head, part_fgain) = scatter_all(
        (b_b, a_b, att_b, dbr_b), (dup_b, dqkv_b, dat_b, hid_b)
    )
    total_sq = spread_sum(squares)
    part_in = after(piece, total_sq)
    for bit in reversed(bits[:-1]):
        up = (dp_index // bit) % 2 == 1
        other = moved(part_in, flip_dp(bit))
        part_in = jnp.concatenate([jnp.where(up, other, part_in), jnp.where(up, part_in, other)])
    part_in = part_in.astype(F32)
    total_sq = total_sq[0, 0]
    shard_wide = shards[None]
    grow = 1.0 / (shrink * count)
    grad_norm = jnp.sqrt(total_sq) * grow
    factor = CLIP / jnp.maximum(grad_norm, CLIP) * grow
    mats_out = adam(mats, shard_wide * factor, mats_m, mats_v, RATE, DECAY)
    gains_out = adam(gains, sum_gain[None] * factor, gains_m, gains_v, RATE_GAIN, 0.0)
    fgain_out = adam(final_gain, part_fgain * factor, fgain_m, fgain_v, RATE_GAIN, 0.0)
    in_out = adam(w_in, part_in * factor, win_m, win_v, RATE, DECAY)
    head_out = adam(head, part_head * factor, head_m, head_v, RATE, DECAY)
    return (
        grad_norm,
        loss_sum,
        count,
        mats_out[0],
        mats_out[1],
        mats_out[2],
        gains_out[0],
        gains_out[1],
        gains_out[2],
        fgain_out[0],
        fgain_out[1],
        fgain_out[2],
        in_out[0],
        in_out[1],
        in_out[2],
        head_out[0],
        head_out[1],
        head_out[2],
    )


def solution(mesh):
    placed = (
        P("dp", None, None),
        P("dp", None),
        P(None, "dp", None),
        P("dp", None, None),
        P("dp", None, None),
        P("section", None, "dp", None),
        P("section", None, "dp", None),
        P("section", None, "dp", None),
        P("section", None, None),
        P("section", None, None),
        P("section", None, None),
        P("section"),
        P("section"),
        P("section"),
        P("section", None),
        P("section", None),
        P("section", None),
        P("section", None),
        P("section", None),
        P("section", None),
    )
    return jax.shard_map(
        per_device,
        mesh=mesh,
        in_specs=placed,
        out_specs=(
            P(),
            P(),
            P(),
            P("section", None, "dp", None),
            P("section", None, "dp", None),
            P("section", None, "dp", None),
            P("section", None, None),
            P("section", None, None),
            P("section", None, None),
            P("section"),
            P("section"),
            P("section"),
            P("section", None),
            P("section", None),
            P("section", None),
            P("section", None),
            P("section", None),
            P("section", None),
        ),
        check_vma=False,
    )
```

profile of v0, /device:TPU:0, one launch (start us, length us, event | category | flops | bytes accessed | tf_op | source)
XLA Modules:
  0.0 534.2 jit_solution(14723052227256197510)
XLA Ops:
  21.3 5.3 multiply_sine_fusion.1
  26.6 6.5 %collective-permute-done.9 = bf16[1,416,768]{2,1,0:T(8,128)(2,1)} collective-permute-done((bf16[1,416,768]{2,1,0:T(8,128)(2,1)S(1)}, bf16[1,416,768]{2,1,0:T(8,128)(2,1)}, u32[]{:S(2)}, u32[]{:S(2)}) %collective-permute-start.9) | collective-permute-done | bytes 639008 | tf_op jit(solution)/shard_map/ppermute | solution.py:32
  35.5 18.4 %collective-permute-done.2.refs_2_ = bf16[2,3,48,3072]{3,2,1,0:T(8,128)(2,1)} collective-permute-done((bf16[2,3,48,3072]{3,2,1,0:T(8,128)(2,1)}, bf16[2,3,48,3072]{3,2,1,0:T(8,128)(2,1)}, u32[]{:S(2)}, u32[]{:S(2)}) %collective-permute-start.2) | collective-permute-done | bytes 1769504 | tf_op jit(solution)/shard_map/ppermute | solution.py:32
  72.3 11.1 %collective-permute-done.5.refs_3_ = bf16[3,48,3072]{2,1,0:T(8,128)(2,1)} collective-permute-done((bf16[3,48,3072]{2,1,0:T(8,128)(2,1)}, bf16[3,48,3072]{2,1,0:T(8,128)(2,1)}, u32[]{:S(2)}, u32[]{:S(2)}) %collective-permute-start.5) | collective-permute-done | bytes 884768 | tf_op jit(solution)/shard_map/ppermute | solution.py:32
  96.8 9.1 %collective-permute-start.17 = (bf16[3,48,3072]{2,1,0:T(8,128)(2,1)}, bf16[3,48,3072]{2,1,0:T(8,128)(2,1)}, u32[]{:S(2)}, u32[]{:S(2)}) collective-permute-start(bf16[3,48,3072]{2,1,0:T(8,128)(2,1)} %collective-permute-done.5.refs_3_), channel_id=1, source_target_pairs={{0,1},{3,2},{4,5},{7,6},{8,9},{11,10},{12,13},{15,14},{17,16},{18,... | collective-permute-start | bytes 2654216 | tf_op jit(solution)/shard_map/ppermute | solution.py:32
  111.6 7.2 %collective-permute-start.11 = (s32[2,236]{1,0:T(2,128)S(1)}, s32[2,236]{1,0:T(2,128)S(1)}, u32[]{:S(2)}, u32[]{:S(2)}) collective-permute-start(s32[2,236]{1,0:T(2,128)S(1)} %fusion.22), channel_id=1, source_target_pairs={{0,16},{1,17},{2,18},{3,19},{4,20},{5,21},{6,22},{7,23},{8,24},{9,... | collective-permute-start | bytes 5672 | tf_op jit(solution)/shard_map/ppermute | solution.py:32
  125.7 8.2 %load_weights.1 = (bf16[768,2304]{1,0:T(8,128)(2,1)S(1)}, bf16[768,768]{1,0:T(8,128)(2,1)S(1)}, bf16[768,3072]{1,0:T(8,128)(2,1)S(1)}, bf16[768,3072]{1,0:T(8,12...) custom-call(s32[17]{0:T(128)S(1)} %stack.437.scal, ...), custom_call_target="tpu_custom_call" | custom-call | tf_op jit(solution)/shard_map/load_weights/pallas_call | solution.py:443
  134.0 8.3 %layer_forward.10 = (bf16[128,768]{1,0:T(8,128)(2,1)S(1)}, bf16[4,128,768]{2,1,0:T(8,128)(2,1)}, bf16[4,128,2304]{2,1,0:T(8,128)(2,1)}, f32[4,16,128]{2,1,0:T(8,...) custom-call(s32[4]{0:T(128)S(1)} %get-tuple-element.674.refs_0_, ...), custom_call_target="tpu_custom_call" | custom-call | flops 7516192768 | bytes 8388608 | tf_op jit(solution)/shard_map/layer_forward/pallas_call | solution.py:537
  145.4 7.9 %layer_forward.11 = (bf16[128,768]{1,0:T(8,128)(2,1)S(1)}, bf16[4,128,768]{2,1,0:T(8,128)(2,1)}, bf16[4,128,2304]{2,1,0:T(8,128)(2,1)}, f32[4,16,128]{2,1,0:T(8,...) custom-call(s32[4]{0:T(128)S(1)} %get-tuple-element.673.refs_0_, ...), custom_call_target="tpu_custom_call", output_to_operand_aliasing={{1}: (18, {}), {2}: (19, {}), {3}: (20, {}), {4}: (21, {}),... | custom-call | flops 7516192768 | bytes 8388608 | tf_op jit(solution)/shard_map/layer_forward/pallas_call | solution.py:537
  154.6 7.9 %layer_forward.12 = (bf16[128,768]{1,0:T(8,128)(2,1)S(1)}, bf16[4,128,768]{2,1,0:T(8,128)(2,1)}, bf16[4,128,2304]{2,1,0:T(8,128)(2,1)}, f32[4,16,128]{2,1,0:T(8,...) custom-call(s32[4]{0:T(128)S(1)} %add_add_fusion.6.refs_0_, ...), custom_call_target="tpu_custom_call", output_to_operand_aliasing={{1}: (18, {}), {2}: (19, {}), {3}: (20, {}), {4}: (21, {}),... | custom-call | flops 7516192768 | bytes 8388608 | tf_op jit(solution)/shard_map/layer_forward/pallas_call | solution.py:537
  163.8 8.5 %layer_forward.13 = (bf16[128,768]{1,0:T(8,128)(2,1)S(1)}, bf16[4,128,768]{2,1,0:T(8,128)(2,1)}, bf16[4,128,2304]{2,1,0:T(8,128)(2,1)}, f32[4,16,128]{2,1,0:T(8,...) custom-call(s32[4]{0:T(128)S(1)} %add_add_fusion.5.refs_0_, ...), custom_call_target="tpu_custom_call", output_to_operand_aliasing={{1}: (18, {}), {2}: (19, {}), {3}: (20, {}), {4}: (21, {}),... | custom-call | flops 7516192768 | bytes 8388608 | tf_op jit(solution)/shard_map/layer_forward/pallas_call | solution.py:537
  177.6 11.7 %collective-permute-start.29 = (bf16[128,768]{1,0:T(8,128)(2,1)S(1)}, bf16[128,768]{1,0:T(8,128)(2,1)S(1)}, u32[]{:S(2)}, u32[]{:S(2)}) collective-permute-start(bf16[128,768]{1,0:T(8,128)(2,1)S(1)} %get-tuple-element.441), channel_id=1, source_target_pairs={{0,16},{1,17},{4,20},{5,21},{8,24},{9,25},{12,28},{13,29},{16,18},... | collective-permute-start | bytes 589832 | tf_op jit(solution)/shard_map/ppermute | solution.py:32
  190.0 10.6 %collective-permute-start.28 = (bf16[128,768]{1,0:T(8,128)(2,1)S(1)}, bf16[128,768]{1,0:T(8,128)(2,1)S(1)}, u32[]{:S(2)}, u32[]{:S(2)}) collective-permute-start(bf16[128,768]{1,0:T(8,128)(2,1)S(1)} %get-tuple-element.440), channel_id=1, source_target_pairs={{0,16},{1,17},{4,20},{5,21},{8,24},{9,25},{12,28},{13,29},{16,18},... | collective-permute-start | bytes 589832 | tf_op jit(solution)/shard_map/ppermute | solution.py:32
  200.6 7.5 %layer_forward.16 = (bf16[128,768]{1,0:T(8,128)(2,1)S(1)}, bf16[4,128,768]{2,1,0:T(8,128)(2,1)}, bf16[4,128,2304]{2,1,0:T(8,128)(2,1)}, f32[4,16,128]{2,1,0:T(8,...) custom-call(s32[4]{0:T(128)S(1)} %add_add_fusion.8.refs_0_, ...), custom_call_target="tpu_custom_call", output_to_operand_aliasing={{1}: (18, {}), {2}: (19, {}), {3}: (20, {}), {4}: (21, {}),... | custom-call | flops 7516192768 | bytes 8388608 | tf_op jit(solution)/shard_map/layer_forward/pallas_call | solution.py:537
  218.2 9.2 %layer_forward.19 = (bf16[128,768]{1,0:T(8,128)(2,1)}, bf16[4,128,768]{2,1,0:T(8,128)(2,1)}, bf16[4,128,2304]{2,1,0:T(8,128)(2,1)}, f32[4,16,128]{2,1,0:T(8,128)...) custom-call(s32[4]{0:T(128)S(1)} %add_add_fusion.refs_0_, ...), custom_call_target="tpu_custom_call", output_to_operand_aliasing={{1}: (18, {}), {2}: (19, {}), {3}: (20, {}), {4}: (21, {}),... | custom-call | flops 7516192768 | bytes 8388608 | tf_op jit(solution)/shard_map/layer_forward/pallas_call | solution.py:537
  231.2 19.4 %collective-permute-done.33.refs_3_ = bf16[128,768]{1,0:T(8,128)(2,1)S(1)} collective-permute-done((bf16[128,768]{1,0:T(8,128)(2,1)S(1)}, bf16[128,768]{1,0:T(8,128)(2,1)S(1)}, u32[]{:S(2)}, u32[]{:S(2)}) %collective-permute-start.33) | collective-permute-done | bytes 196640 | tf_op jit(solution)/shard_map/ppermute | solution.py:32
  250.6 8.3 %layer_backward.12 = (bf16[128,768]{1,0:T(8,128)(2,1)S(1)}, bf16[4,128,768]{2,1,0:T(8,128)(2,1)S(1)}, bf16[4,128,3072]{2,1,0:T(8,128)(2,1)S(1)}, bf16[4,128,768]...) custom-call(s32[4]{0:T(128)S(1)} %add_add_fusion.16.refs_0_, ...), custom_call_target="tpu_custom_call", output_to_operand_aliasing={{1}: (15, {}), {2}: (16, {}), {3}: (17, {}), {4}: (18, {}),... | custom-call | flops 10737418240 | bytes 8388608 | tf_op jit(solution)/shard_map/layer_backward/pallas_call | solution.py:571
  262.1 8.1 %collective-permute-done.35.refs_3_ = bf16[128,768]{1,0:T(8,128)(2,1)S(1)} collective-permute-done((bf16[128,768]{1,0:T(8,128)(2,1)S(1)}, bf16[128,768]{1,0:T(8,128)(2,1)S(1)}, u32[]{:S(2)}, u32[]{:S(2)}) %collective-permute-start.35) | collective-permute-done | bytes 196640 | tf_op jit(solution)/shard_map/ppermute | solution.py:32
  272.3 8.5 %layer_backward.15 = (bf16[128,768]{1,0:T(8,128)(2,1)S(1)}, bf16[4,128,768]{2,1,0:T(8,128)(2,1)S(1)}, bf16[4,128,3072]{2,1,0:T(8,128)(2,1)S(1)}, bf16[4,128,768]...) custom-call(s32[4]{0:T(128)S(1)} %add_add_fusion.12.refs_0_, ...), custom_call_target="tpu_custom_call", output_to_operand_aliasing={{1}: (15, {}), {2}: (16, {}), {3}: (17, {}), {4}: (18, {}),... | custom-call | flops 10737418240 | bytes 8388608 | tf_op jit(solution)/shard_map/layer_backward/pallas_call | solution.py:571
  286.2 8.8 %layer_backward.16 = (bf16[128,768]{1,0:T(8,128)(2,1)S(1)}, bf16[4,128,768]{2,1,0:T(8,128)(2,1)S(1)}, bf16[4,128,3072]{2,1,0:T(8,128)(2,1)S(1)}, bf16[4,128,768]...) custom-call(s32[4]{0:T(128)S(1)} %add_add_fusion.18.refs_0_, ...), custom_call_target="tpu_custom_call", output_to_operand_aliasing={{1}: (15, {}), {2}: (16, {}), {3}: (17, {}), {4}: (18, {}),... | custom-call | flops 10737418240 | bytes 8388608 | tf_op jit(solution)/shard_map/layer_backward/pallas_call | solution.py:571
  297.2 8.8 %layer_backward.17 = (bf16[128,768]{1,0:T(8,128)(2,1)S(1)}, bf16[4,128,768]{2,1,0:T(8,128)(2,1)S(1)}, bf16[4,128,3072]{2,1,0:T(8,128)(2,1)S(1)}, bf16[4,128,768]...) custom-call(s32[4]{0:T(128)S(1)} %add_add_fusion.11.refs_0_, ...), custom_call_target="tpu_custom_call", output_to_operand_aliasing={{1}: (15, {}), {2}: (16, {}), {3}: (17, {}), {4}: (18, {}),... | custom-call | flops 10737418240 | bytes 8388608 | tf_op jit(solution)/shard_map/layer_backward/pallas_call | solution.py:571
  307.9 9.7 %layer_backward.18 = (bf16[128,768]{1,0:T(8,128)(2,1)S(1)}, bf16[4,128,768]{2,1,0:T(8,128)(2,1)S(1)}, bf16[4,128,3072]{2,1,0:T(8,128)(2,1)S(1)}, bf16[4,128,768]...) custom-call(s32[4]{0:T(128)S(1)} %add_add_fusion.19.refs_0_, ...), custom_call_target="tpu_custom_call", output_to_operand_aliasing={{1}: (15, {}), {2}: (16, {}), {3}: (17, {}), {4}: (18, {}),... | custom-call | flops 10737418240 | bytes 8388608 | tf_op jit(solution)/shard_map/layer_backward/pallas_call | solution.py:571
  317.6 8.8 %layer_backward.19 = (bf16[128,768]{1,0:T(8,128)(2,1)S(1)}, bf16[4,128,768]{2,1,0:T(8,128)(2,1)S(1)}, bf16[4,128,3072]{2,1,0:T(8,128)(2,1)S(1)}, bf16[4,128,768]...) custom-call(s32[4]{0:T(128)S(1)} %add_add_fusion.10.refs_0_, ...), custom_call_target="tpu_custom_call", output_to_operand_aliasing={{1}: (15, {}), {2}: (16, {}), {3}: (17, {}), {4}: (18, {}),... | custom-call | flops 10737418240 | bytes 8388608 | tf_op jit(solution)/shard_map/layer_backward/pallas_call | solution.py:571
  326.5 13.0 %weight_grads.1 = (bf16[3,96,3072]{2,1,0:T(8,128)(2,1)}, bf16[3,288,3072]{2,1,0:T(8,128)(2,1)}, bf16[3,384,3072]{2,1,0:T(8,128)(2,1)}) custom-call(s32[8]{0:T(128)S(1)} %stack.405.order, bf16[4,128,768]{2,1,0:T(8,128)(2,1)} %get-tuple-element.496.refs_0_, bf16[4,128,768]{2,1,0:T(8,128)(2,1)} %get-tuple-element.497.refs_1_, ...), custom_call_target="tpu_custom_call" | custom-call | flops 7247757312 | bytes 28311552 | tf_op jit(solution)/shard_map/weight_grads/pallas_call | solution.py:501
  368.2 5.5 %collective-permute-done.42 = bf16[3,48,3072]{2,1,0:T(8,128)(2,1)} collective-permute-done((bf16[3,48,3072]{2,1,0:T(8,128)(2,1)}, bf16[3,48,3072]{2,1,0:T(8,128)(2,1)}, u32[]{:S(2)}, u32[]{:S(2)}) %collective-permute-start.42) | collective-permute-done | bytes 884768 | tf_op jit(solution)/shard_map/ppermute | solution.py:32
  387.4 9.5 %collective-permute-done.51 = f32[16384]{0:T(1024)S(1)} collective-permute-done((f32[16384]{0:T(1024)S(1)}, f32[16384]{0:T(1024)S(1)}, u32[]{:S(2)}, u32[]{:S(2)}) %collective-permute-start.51) | collective-permute-done | bytes 65568 | tf_op jit(solution)/shard_map/ppermute | solution.py:32
  402.5 5.5 %collective-permute-done.53 = f32[16384]{0:T(1024)S(1)} collective-permute-done((f32[16384]{0:T(1024)S(1)}, f32[16384]{0:T(1024)S(1)}, u32[]{:S(2)}, u32[]{:S(2)}) %collective-permute-start.53) | collective-permute-done | bytes 65568 | tf_op jit(solution)/shard_map/ppermute | solution.py:32
  409.0 5.5 %fusion.5 = bf16[3,96,3072]{2,1,0:T(8,128)(2,1)} fusion(bf16[3,96,3072]{2,1,0:T(8,128)(2,1)} %collective-permute-done.45, bf16[3,96,3072]{2,1,0:T(8,128)(2,1)} %collective-permute-done.44, bf16[3,4,96,3072]{3,2,1,0:T(8,128)(2,1)} %bitcast.216, bf16[3,3,96,3072]{3,2,1,0:T(8,128)(2,1)} %bitcast.88), kind=kLoop, calls=%fused_computation.11 | loop fusion | flops 7077888 | bytes 8847360 | tf_op jit(solution)/shard_map/convert_element_type | solution.py:803
  426.0 13.3 %collective-permute-done.56 = bf16[3,96,3072]{2,1,0:T(8,128)(2,1)} collective-permute-done((bf16[3,96,3072]{2,1,0:T(8,128)(2,1)}, bf16[3,96,3072]{2,1,0:T(8,128)(2,1)}, u32[]{:S(2)}, u32[]{:S(2)}) %collective-permute-start.56) | collective-permute-done | bytes 1769504 | tf_op jit(solution)/shard_map/ppermute | solution.py:32
  439.2 8.8 %collective-permute-done.57 = bf16[3,96,3072]{2,1,0:T(8,128)(2,1)} collective-permute-done((bf16[3,96,3072]{2,1,0:T(8,128)(2,1)S(1)}, bf16[3,96,3072]{2,1,0:T(8,128)(2,1)}, u32[]{:S(2)}, u32[]{:S(2)}) %collective-permute-start.57) | collective-permute-done | bytes 1769504 | tf_op jit(solution)/shard_map/ppermute | solution.py:32
  466.1 14.5 %collective-permute-done.61 = f32[2,768]{1,0:T(2,128)} collective-permute-done((f32[2,768]{1,0:T(2,128)}, f32[2,768]{1,0:T(2,128)}, u32[]{:S(2)}, u32[]{:S(2)}) %collective-permute-start.61) | collective-permute-done | bytes 6176 | tf_op jit(solution)/shard_map/ppermute | solution.py:32
  513.5 8.2 %multiply_subtract_fusion = (f32[1,3,96,3072]{3,2,1,0:T(8,128)}, f32[1,3,96,3072]{3,2,1,0:T(8,128)}, f32[1,3,96,3072]{3,2,1,0:T(8,128)}) fusion(f32[1,3,96,3072]{3,2,1,0:T(8,128)} %param.25, f32[]{:T(128)S(6)} %mul.464, bf16[3,96,3072]{2,1,0:T(8,128)(2,1)S(1)} %fusion.7, bf16[3,96,3072]{2,1,0:T(8,128)(2,1)} %collective-permute-done.55, pred[]{:T(512)S(6)} %eq.198, ...), kind=kLoop, calls=%fused_computation.14 | loop fusion | flops 15925248 | bytes 24772612 | tf_op jit(solution)/shard_map/sub | solution.py:614
  (341 shorter events, 220.5 us)
Async XLA Ops:
  4.4 31.1 %collective-permute-start = (bf16[2,3,48,3072]{3,2,1,0:T(8,128)(2,1)}, bf16[2,3,48,3072]{3,2,1,0:T(8,128)(2,1)}, u32[]{:S(2)}, u32[]{:S(2)}) collective-permute-start(bf16[2,3,48,3072]{3,2,1,0:T(8,128)(2,1)} %bitcast.209.refs_0_), channel_id=1, source_target_pairs={{1,16},{2,19},{5,20},{6,23},{9,24},{10,27},{13,28},{14,31},{16,1},... | collective-permute-start | bytes 5308424 | tf_op jit(solution)/shard_map/ppermute | solution.py:32
  6.5 29.0 %collective-permute-start.1 = (bf16[2,3,48,3072]{3,2,1,0:T(8,128)(2,1)}, bf16[2,3,48,3072]{3,2,1,0:T(8,128)(2,1)}, u32[]{:S(2)}, u32[]{:S(2)}) collective-permute-start(bf16[2,3,48,3072]{3,2,1,0:T(8,128)(2,1)} %bitcast.209.refs_0_), channel_id=1, source_target_pairs={{0,4},{3,7},{4,0},{7,3},{8,12},{11,15},{12,8},{15,11},{17,21},{18,... | collective-permute-start | bytes 5308424 | tf_op jit(solution)/shard_map/ppermute | solution.py:32
  11.3 42.6 %collective-permute-start.2 = (bf16[2,3,48,3072]{3,2,1,0:T(8,128)(2,1)}, bf16[2,3,48,3072]{3,2,1,0:T(8,128)(2,1)}, u32[]{:S(2)}, u32[]{:S(2)}) collective-permute-start(bf16[2,3,48,3072]{3,2,1,0:T(8,128)(2,1)} %bitcast.209.refs_0_), channel_id=1, source_target_pairs={{0,8},{3,11},{4,12},{7,15},{8,0},{11,3},{12,4},{15,7},{17,25},{18,... | collective-permute-start | bytes 5308424 | tf_op jit(solution)/shard_map/ppermute | solution.py:32
  14.8 50.5 %collective-permute-start.7 = (bf16[2,3,48,3072]{3,2,1,0:T(8,128)(2,1)}, bf16[2,3,48,3072]{3,2,1,0:T(8,128)(2,1)}, u32[]{:S(2)}, u32[]{:S(2)}) collective-permute-start(bf16[2,3,48,3072]{3,2,1,0:T(8,128)(2,1)} %bitcast.209.refs_0_), channel_id=1, source_target_pairs={{0,1},{3,2},{4,5},{7,6},{8,9},{11,10},{12,13},{15,14},{17,16},{18,... | collective-permute-start | bytes 5308424 | tf_op jit(solution)/shard_map/ppermute | solution.py:32
  34.3 28.9 %collective-permute-start.10 = (bf16[2,1,416,768]{3,2,1,0:T(8,128)(2,1)S(1)}, bf16[2,1,416,768]{3,2,1,0:T(8,128)(2,1)S(1)}, u32[]{:S(2)}, u32[]{:S(2)}) collective-permute-start(bf16[2,1,416,768]{3,2,1,0:T(8,128)(2,1)S(1)} %pad_maximum_fusion), channel_id=1, source_target_pairs={{0,1},{1,0},{2,3},{3,2},{4,5},{5,4},{6,7},{7,6},{8,9},{9,8},{10,11... | collective-permute-start | bytes 3833864 | tf_op jit(solution)/shard_map/ppermute | solution.py:32
  53.9 34.3 %collective-permute-start.3 = (bf16[2,3,48,3072]{3,2,1,0:T(8,128)(2,1)}, bf16[2,3,48,3072]{3,2,1,0:T(8,128)(2,1)}, u32[]{:S(2)}, u32[]{:S(2)}) collective-permute-start(bf16[2,3,48,3072]{3,2,1,0:T(8,128)(2,1)} %collective-permute-done.refs_10_), channel_id=1, source_target_pairs={{1,5},{2,6},{5,1},{6,2},{9,13},{10,14},{13,9},{14,10},{16,20},{19,... | collective-permute-start | bytes 5308424 | tf_op jit(solution)/shard_map/ppermute | solution.py:32
  55.8 32.6 %collective-permute-start.4 = (bf16[2,3,48,3072]{3,2,1,0:T(8,128)(2,1)}, bf16[2,3,48,3072]{3,2,1,0:T(8,128)(2,1)}, u32[]{:S(2)}, u32[]{:S(2)}) collective-permute-start(bf16[2,3,48,3072]{3,2,1,0:T(8,128)(2,1)} %collective-permute-done.refs_10_), channel_id=1, source_target_pairs={{1,9},{2,10},{5,13},{6,14},{9,1},{10,2},{13,5},{14,6},{16,24},{19,... | collective-permute-start | bytes 5308424 | tf_op jit(solution)/shard_map/ppermute | solution.py:32
  57.7 30.7 %collective-permute-start.8 = (bf16[2,3,48,3072]{3,2,1,0:T(8,128)(2,1)}, bf16[2,3,48,3072]{3,2,1,0:T(8,128)(2,1)}, u32[]{:S(2)}, u32[]{:S(2)}) collective-permute-start(bf16[2,3,48,3072]{3,2,1,0:T(8,128)(2,1)} %collective-permute-done.refs_10_), channel_id=1, source_target_pairs={{1,0},{2,3},{5,4},{6,7},{9,8},{10,11},{13,12},{14,15},{16,17},{19,... | collective-permute-start | bytes 5308424 | tf_op jit(solution)/shard_map/ppermute | solution.py:32
  63.2 20.2 %collective-permute-start.5 = (bf16[3,48,3072]{2,1,0:T(8,128)(2,1)}, bf16[3,48,3072]{2,1,0:T(8,128)(2,1)}, u32[]{:S(2)}, u32[]{:S(2)}) collective-permute-start(bf16[3,48,3072]{2,1,0:T(8,128)(2,1)} %slice_bitcast_fusion.11), channel_id=1, source_target_pairs={{0,4},{3,7},{4,0},{7,3},{8,12},{11,15},{12,8},{15,11},{17,21},{18,... | collective-permute-start | bytes 2654216 | tf_op jit(solution)/shard_map/ppermute | solution.py:32
  65.3 21.2 %collective-permute-start.6 = (bf16[3,48,3072]{2,1,0:T(8,128)(2,1)}, bf16[3,48,3072]{2,1,0:T(8,128)(2,1)}, u32[]{:S(2)}, u32[]{:S(2)}) collective-permute-start(bf16[3,48,3072]{2,1,0:T(8,128)(2,1)} %slice_bitcast_fusion.10), channel_id=1, source_target_pairs={{0,8},{3,11},{4,12},{7,15},{8,0},{11,3},{12,4},{15,7},{17,25},{18,... | collective-permute-start | bytes 2654216 | tf_op jit(solution)/shard_map/ppermute | solution.py:32
  89.6 29.1 %collective-permute-start.20 = (bf16[2,3,48,3072]{3,2,1,0:T(8,128)(2,1)}, bf16[2,3,48,3072]{3,2,1,0:T(8,128)(2,1)}, u32[]{:S(2)}, u32[]{:S(2)}) collective-permute-start(bf16[2,3,48,3072]{3,2,1,0:T(8,128)(2,1)} %collective-permute-done.4.refs_12_), channel_id=1, source_target_pairs={{1,0},{2,3},{5,4},{6,7},{9,8},{10,11},{13,12},{14,15},{16,17},{19,... | collective-permute-start | bytes 5308424 | tf_op jit(solution)/shard_map/ppermute | solution.py:32
  91.7 27.1 %collective-permute-start.19 = (bf16[2,3,48,3072]{3,2,1,0:T(8,128)(2,1)}, bf16[2,3,48,3072]{3,2,1,0:T(8,128)(2,1)}, u32[]{:S(2)}, u32[]{:S(2)}) collective-permute-start(bf16[2,3,48,3072]{3,2,1,0:T(8,128)(2,1)} %collective-permute-done.3.refs_11_), channel_id=1, source_target_pairs={{1,0},{2,3},{5,4},{6,7},{9,8},{10,11},{13,12},{14,15},{16,17},{19,... | collective-permute-start | bytes 5308424 | tf_op jit(solution)/shard_map/ppermute | solution.py:32
  95.1 16.5 %collective-permute-start.14 = (bf16[3,48,3072]{2,1,0:T(8,128)(2,1)}, bf16[3,48,3072]{2,1,0:T(8,128)(2,1)}, u32[]{:S(2)}, u32[]{:S(2)}) collective-permute-start(bf16[3,48,3072]{2,1,0:T(8,128)(2,1)} %slice_bitcast_fusion.8), channel_id=1, source_target_pairs={{1,9},{2,10},{5,13},{6,14},{9,1},{10,2},{13,5},{14,6},{16,24},{19,... | collective-permute-start | bytes 2654216 | tf_op jit(solution)/shard_map/ppermute | solution.py:32
  96.8 22.0 %collective-permute-start.17 = (bf16[3,48,3072]{2,1,0:T(8,128)(2,1)}, bf16[3,48,3072]{2,1,0:T(8,128)(2,1)}, u32[]{:S(2)}, u32[]{:S(2)}) collective-permute-start(bf16[3,48,3072]{2,1,0:T(8,128)(2,1)} %collective-permute-done.5.refs_3_), channel_id=1, source_target_pairs={{0,1},{3,2},{4,5},{7,6},{8,9},{11,10},{12,13},{15,14},{17,16},{18,... | collective-permute-start | bytes 2654216 | tf_op jit(solution)/shard_map/ppermute | solution.py:32
  122.6 32.0 %collective-permute-start.23 = (bf16[2,128,768]{2,1,0:T(8,128)(2,1)S(1)}, bf16[2,128,768]{2,1,0:T(8,128)(2,1)S(1)}, u32[]{:S(2)}, u32[]{:S(2)}) collective-permute-start(bf16[2,128,768]{2,1,0:T(8,128)(2,1)S(1)} %constant_dynamic-slice_fusion.3), channel_id=1, source_target_pairs={{16,0},{17,1},{20,4},{21,5},{24,8},{25,9},{28,12},{29,13}} | collective-permute-start | bytes 1179656 | tf_op jit(solution)/shard_map/ppermute | solution.py:32
  172.3 17.0 %collective-permute-start.26 = (bf16[128,768]{1,0:T(8,128)(2,1)S(1)}, bf16[128,768]{1,0:T(8,128)(2,1)S(1)}, u32[]{:S(2)}, u32[]{:S(2)}) collective-permute-start(bf16[128,768]{1,0:T(8,128)(2,1)S(1)} %get-tuple-element.412), channel_id=1, source_target_pairs={{0,16},{1,17},{4,20},{5,21},{8,24},{9,25},{12,28},{13,29},{16,18},... | collective-permute-start | bytes 589832 | tf_op jit(solution)/shard_map/ppermute | solution.py:32
  177.6 23.1 %collective-permute-start.29 = (bf16[128,768]{1,0:T(8,128)(2,1)S(1)}, bf16[128,768]{1,0:T(8,128)(2,1)S(1)}, u32[]{:S(2)}, u32[]{:S(2)}) collective-permute-start(bf16[128,768]{1,0:T(8,128)(2,1)S(1)} %get-tuple-element.441), channel_id=1, source_target_pairs={{0,16},{1,17},{4,20},{5,21},{8,24},{9,25},{12,28},{13,29},{16,18},... | collective-permute-start | bytes 589832 | tf_op jit(solution)/shard_map/ppermute | solution.py:32
  190.0 20.1 %collective-permute-start.28 = (bf16[128,768]{1,0:T(8,128)(2,1)S(1)}, bf16[128,768]{1,0:T(8,128)(2,1)S(1)}, u32[]{:S(2)}, u32[]{:S(2)}) collective-permute-start(bf16[128,768]{1,0:T(8,128)(2,1)S(1)} %get-tuple-element.440), channel_id=1, source_target_pairs={{0,16},{1,17},{4,20},{5,21},{8,24},{9,25},{12,28},{13,29},{16,18},... | collective-permute-start | bytes 589832 | tf_op jit(solution)/shard_map/ppermute | solution.py:32
  228.0 22.6 %collective-permute-start.33 = (bf16[128,768]{1,0:T(8,128)(2,1)S(1)}, bf16[128,768]{1,0:T(8,128)(2,1)S(1)}, u32[]{:S(2)}, u32[]{:S(2)}) collective-permute-start(bf16[128,768]{1,0:T(8,128)(2,1)S(1)} %get-tuple-element.511), channel_id=1, source_target_pairs={{2,18},{3,19},{6,22},{7,23},{10,26},{11,27},{14,30},{15,31},{16,0}... | collective-permute-start | bytes 589832 | tf_op jit(solution)/shard_map/ppermute | solution.py:32
  229.9 30.3 %collective-permute-start.32 = (bf16[128,768]{1,0:T(8,128)(2,1)S(1)}, bf16[128,768]{1,0:T(8,128)(2,1)S(1)}, u32[]{:S(2)}, u32[]{:S(2)}) collective-permute-start(bf16[128,768]{1,0:T(8,128)(2,1)S(1)} %get-tuple-element.510), channel_id=1, source_target_pairs={{2,18},{3,19},{6,22},{7,23},{10,26},{11,27},{14,30},{15,31},{16,0}... | collective-permute-start | bytes 589832 | tf_op jit(solution)/shard_map/ppermute | solution.py:32
  280.7 16.4 %collective-permute-start.36 = (bf16[128,768]{1,0:T(8,128)(2,1)S(1)}, bf16[128,768]{1,0:T(8,128)(2,1)S(1)}, u32[]{:S(2)}, u32[]{:S(2)}) collective-permute-start(bf16[128,768]{1,0:T(8,128)(2,1)S(1)} %get-tuple-element.534), channel_id=1, source_target_pairs={{2,18},{3,19},{6,22},{7,23},{10,26},{11,27},{14,30},{15,31},{16,0}... | collective-permute-start | bytes 589832 | tf_op jit(solution)/shard_map/ppermute | solution.py:32
  343.6 30.8 %collective-permute-start.41 = (bf16[3,288,3072]{2,1,0:T(8,128)(2,1)}, bf16[3,288,3072]{2,1,0:T(8,128)(2,1)}, u32[]{:S(2)}, u32[]{:S(2)}) collective-permute-start(bf16[3,288,3072]{2,1,0:T(8,128)(2,1)} %get-tuple-element.566), channel_id=1, source_target_pairs={{0,1},{1,0},{2,3},{3,2},{4,5},{5,4},{6,7},{7,6},{8,9},{9,8},{10,11... | collective-permute-start | bytes 15925256 | tf_op jit(solution)/shard_map/ppermute | solution.py:32
  351.4 22.2 %collective-permute-start.42 = (bf16[3,48,3072]{2,1,0:T(8,128)(2,1)}, bf16[3,48,3072]{2,1,0:T(8,128)(2,1)}, u32[]{:S(2)}, u32[]{:S(2)}) collective-permute-start(bf16[3,48,3072]{2,1,0:T(8,128)(2,1)} %get-tuple-element.567), channel_id=1, source_target_pairs={{0,4},{1,5},{2,6},{3,7},{4,0},{5,1},{6,2},{7,3},{8,12},{9,13},{10,... | collective-permute-start | bytes 2654216 | tf_op jit(solution)/shard_map/ppermute | solution.py:32
  352.4 21.9 %collective-permute-start.43 = (bf16[3,48,3072]{2,1,0:T(8,128)(2,1)}, bf16[3,48,3072]{2,1,0:T(8,128)(2,1)}, u32[]{:S(2)}, u32[]{:S(2)}) collective-permute-start(bf16[3,48,3072]{2,1,0:T(8,128)(2,1)} %get-tuple-element.568), channel_id=1, source_target_pairs={{0,8},{1,9},{2,10},{3,11},{4,12},{5,13},{6,14},{7,15},{8,0},{9,1},... | collective-permute-start | bytes 2654216 | tf_op jit(solution)/shard_map/ppermute | solution.py:32
  379.5 29.5 %collective-permute-start.44 = (bf16[3,96,3072]{2,1,0:T(8,128)(2,1)}, bf16[3,96,3072]{2,1,0:T(8,128)(2,1)}, u32[]{:S(2)}, u32[]{:S(2)}) collective-permute-start(bf16[3,96,3072]{2,1,0:T(8,128)(2,1)} %get-tuple-element.589), channel_id=1, source_target_pairs={{1,5},{2,6},{5,1},{6,2},{9,13},{10,14},{13,9},{14,10},{16,20},{19,... | collective-permute-start | bytes 5308424 | tf_op jit(solution)/shard_map/ppermute | solution.py:32
  381.3 27.7 %collective-permute-start.45 = (bf16[3,96,3072]{2,1,0:T(8,128)(2,1)S(1)}, bf16[3,96,3072]{2,1,0:T(8,128)(2,1)}, u32[]{:S(2)}, u32[]{:S(2)}) collective-permute-start(bf16[3,96,3072]{2,1,0:T(8,128)(2,1)S(1)} %get-tuple-element.590), channel_id=1, source_target_pairs={{1,9},{2,10},{5,13},{6,14},{9,1},{10,2},{13,5},{14,6},{16,24},{19,... | collective-permute-start | bytes 5308424 | tf_op jit(solution)/shard_map/ppermute | solution.py:32
  414.5 24.7 %collective-permute-start.56 = (bf16[3,96,3072]{2,1,0:T(8,128)(2,1)}, bf16[3,96,3072]{2,1,0:T(8,128)(2,1)}, u32[]{:S(2)}, u32[]{:S(2)}) collective-permute-start(bf16[3,96,3072]{2,1,0:T(8,128)(2,1)} %get-tuple-element.589), channel_id=1, source_target_pairs={{0,4},{3,7},{4,0},{7,3},{8,12},{11,15},{12,8},{15,11},{17,21},{18,... | collective-permute-start | bytes 5308424 | tf_op jit(solution)/shard_map/ppermute | solution.py:32
  417.4 30.6 %collective-permute-start.57 = (bf16[3,96,3072]{2,1,0:T(8,128)(2,1)S(1)}, bf16[3,96,3072]{2,1,0:T(8,128)(2,1)}, u32[]{:S(2)}, u32[]{:S(2)}) collective-permute-start(bf16[3,96,3072]{2,1,0:T(8,128)(2,1)S(1)} %get-tuple-element.590), channel_id=1, source_target_pairs={{0,8},{3,11},{4,12},{7,15},{8,0},{11,3},{12,4},{15,7},{17,25},{18,... | collective-permute-start | bytes 5308424 | tf_op jit(solution)/shard_map/ppermute | solution.py:32
  421.1 71.5 %collective-permute-start.55 = (bf16[3,96,3072]{2,1,0:T(8,128)(2,1)}, bf16[3,96,3072]{2,1,0:T(8,128)(2,1)}, u32[]{:S(2)}, u32[]{:S(2)}) collective-permute-start(bf16[3,96,3072]{2,1,0:T(8,128)(2,1)} %fusion.5), channel_id=1, source_target_pairs={{1,16},{2,19},{5,20},{6,23},{9,24},{10,27},{13,28},{14,31},{16,1},... | collective-permute-start | bytes 5308424 | tf_op jit(solution)/shard_map/ppermute | solution.py:32
  456.0 24.6 %collective-permute-start.61 = (f32[2,768]{1,0:T(2,128)}, f32[2,768]{1,0:T(2,128)}, u32[]{:S(2)}, u32[]{:S(2)}) collective-permute-start(f32[2,768]{1,0:T(2,128)} %reshape.551), channel_id=1, source_target_pairs={{0,16},{1,17},{2,18},{3,19},{4,20},{5,21},{6,22},{7,23},{8,24},{9,... | collective-permute-start | bytes 18440 | tf_op jit(solution)/shard_map/ppermute | solution.py:32
  456.0 33.7 %collective-permute-start.58 = (bf16[96,768]{1,0:T(8,128)(2,1)S(1)}, bf16[96,768]{1,0:T(8,128)(2,1)}, u32[]{:S(2)}, u32[]{:S(2)}) collective-permute-start(bf16[96,768]{1,0:T(8,128)(2,1)S(1)} %add_convert_fusion.2), channel_id=1, source_target_pairs={{0,16},{1,17},{2,18},{3,19},{4,20},{5,21},{6,22},{7,23},{8,24},{9,... | collective-permute-start | bytes 442376 | tf_op jit(solution)/shard_map/ppermute | solution.py:32
  466.0 16.7 %collective-permute-start.60 = (f32[14720]{0:T(1024)S(1)}, f32[14720]{0:T(1024)S(1)}, u32[]{:S(2)}, u32[]{:S(2)}) collective-permute-start(f32[14720]{0:T(1024)S(1)} %fusion.39), channel_id=1, source_target_pairs={{0,16},{1,17},{2,18},{3,19},{4,20},{5,21},{6,22},{7,23},{8,24},{9,... | collective-permute-start | bytes 176648 | tf_op jit(solution)/shard_map/ppermute | solution.py:32
  (75 other events, 888.2 us)
where the time goes:
time: 544 us; the launch traced here: 534 us
  waiting for transfers between devices  155 us (28%)
  starting transfers between devices  138 us (25%)
  Pallas kernels  129 us (24%)
  other arithmetic  62.6 us (12%)
  local copies, waits for them, and re-layouts  33.1 us (6%)
  between operations  12.4 us (2%)
    ppermute x69, waiting for transfers between devices, moved(): return lax.ppermute(block, ('dp', 'section'), pairs)  155 us
    ppermute x69, starting transfers between devices, moved(): return lax.ppermute(block, ('dp', 'section'), pairs)  138 us
    pallas_call x10, Pallas kernels, backward_call(): pl.pallas_call(functools.partial(backward_body, heads, fresh), out_shape=...  55.4 us
    pallas_call x10, Pallas kernels, forward_call(): pl.pallas_call(functools.partial(forward_body, heads, slides, shrink, fre...  52.6 us
    pallas_call x1, Pallas kernels, weight_grads(): pl.pallas_call(functools.partial(weight_grads_body, (rows, micro, tok)),...  13 us
    sub x5, other arithmetic, adam(): weight - rate * (mhat / (jnp.sqrt(vhat) + ADAM_EPS) + decay * weight)  12.5 us
  transfers between devices with their start and end apart: 69, of which 30 were waited for; matrix products, arithmetic and copies ran while one was open for 16% of the time, Pallas kernels for 18%

commit v1 on v0

--- a/solution.py
+++ b/solution.py
@@ -803,12 +803,11 @@
             return after((both(1) + one.astype(F32) + two.astype(F32)).astype(BF))
 
         second = beside_x(first, side)
-        third = beside_z(second, side)
-        total_far = totalled(False, third)
+        total_far = totalled(False, second)
         away = moved(total_far, layer_turn)
         side, over = lax.optimization_barrier((side, over, total_far))[:2]
         total_own = totalled(True, ())
-        small, piece = beside_last(third, total_own)
+        small, piece = beside_last(beside_z(second, total_own), ())
         squares = jnp.where(
             own_layer,
             jnp.sum(jnp.square(total_own.astype(F32))),
@@ -953,12 +952,11 @@
         )
         mine = lax.dynamic_slice_in_dim(flat(tiles), section * in_rows, in_rows, 1)
         piece = inner(mine, flat(rows_in)).astype(BF)
-        grad_head = jnp.where(on_last, inner(flat(nl_b), flat(dlog_b)), 0.0)[:, :genes]
-        side = jnp.where(on_last, jnp.sum(side_b, 0), 0.0)
-        seen = jnp.pad(jnp.sum(marks[:, 0]).reshape(1), (0, LANES - 1))
-        small = jnp.concatenate(
-            [jnp.sum(gg_b, 0)[:2].reshape(-1), seen, side[0], grad_head.reshape(-1), side[1, :LANES]]
-        )
+        grad_head = jnp.where(on_last, inner(flat(dlog_b), flat(nl_b)), 0.0)[:genes]
+        side = jnp.where(on_last, jnp.sum(side_b, 0), 0.0)[:2]
+        seen = jnp.pad(jnp.sum(marks[:, 0]).reshape(1, 1), ((0, 0), (0, width - 1)))
+        fill = jnp.zeros((-(5 + genes) % 8, width), F32)
+        small = jnp.concatenate([side, grad_head, jnp.sum(gg_b, 0)[:2], seen, fill])
         return small + moved(small, flip_section(1)), piece
 
     def folded(held, bit, mark):
@@ -977,33 +975,31 @@
         small, piece = lax.optimization_barrier((*held, mark))[:2]
         return small, (piece.astype(F32) + moved(piece, flip_dp(bits[-1])).astype(F32)).astype(BF)
 
-    n_gain = 2 * width
     lead = (place == 0) & (core == 0)
 
     def settled(small, piece, squares):
-        layer_gain, ends = small[:n_gain].reshape(2, width), small[n_gain + LANES :]
-        count = jnp.maximum(small[n_gain], 1.0)
-        own_ends = jnp.where(on_last, ends, 0.0)
+        layer_gain = small[2 + genes : 4 + genes]
+        count = jnp.maximum(small[4 + genes, 0], 1.0)
+        own_ends = jnp.where(on_last, small[: 2 + genes], 0.0)
+        kind = jnp.arange(small.shape[0])[:, None]
+        counted = (kind == 0) | ((kind >= 2) & (kind < 4 + genes))
         squares = (
             squares
             + 0.5 * jnp.sum(jnp.square(piece.astype(F32)))
-            + jnp.where(lead, jnp.sum(layer_gain * layer_gain), 0.0)
-            + jnp.where(lead, jnp.sum(own_ends[: width + width * genes] ** 2), 0.0)
+            + jnp.where(lead, jnp.sum(jnp.where(counted, small * small, 0.0)), 0.0)
         )
         sum_gain = jnp.where(own_layer, layer_gain, moved(layer_gain, flip_dp(near)))
         ends = own_ends + moved(own_ends, flip_section(2))
         ends = ends + moved(ends, flip_dp(near))
-        sum_fgain = ends[:width]
-        sum_head = ends[width : width + width * genes].reshape(width, genes)
-        loss_sum = jnp.sum(ends[width + width * genes :])
+        loss_sum = jnp.sum(ends[1, :LANES])
         part = width // sections
-        part_head = lax.dynamic_slice_in_dim(sum_head, section * part, part, 0)
-        part_fgain = lax.dynamic_slice_in_dim(sum_fgain, section * part, part, 0)
-        return squares.reshape(1, 1), piece, count, loss_sum, sum_gain, part_head, part_fgain
-
-    shards, (squares, piece, count, loss_sum, sum_gain, part_head, part_fgain) = scatter_all(
+        mine = lax.dynamic_slice_in_dim(ends, section * part, part, 1)
+        return squares.reshape(1, 1), piece, count, loss_sum, sum_gain, mine
+
+    shards, (squares, piece, count, loss_sum, sum_gain, mine) = scatter_all(
         (b_b, a_b, att_b, dbr_b), (dup_b, dqkv_b, dat_b, hid_b)
     )
+    part_head, part_fgain = mine[2:].T, mine[0]
     total_sq = spread_sum(squares)
     part_in = after(piece, total_sq)
     for bit in reversed(bits[:-1]):

time: 544 us -> 536 us (0.985)
  starting transfers between devices: 138 us -> 157 us
  local copies, waits for them, and re-layouts: 33.1 us -> 16.2 us
    ppermute x69, starting transfers between devices: 138 us -> 157 us  [moved(): return lax.ppermute(block, ('dp', 'section'), pairs)]
    unnamed x81 -> x69, local copies, waits for them, and re-layouts: 7.16 us -> 0.3 us
  transfers between devices with their start and end apart: 69 -> 69, of which waited for: 30 -> 28; matrix products, arithmetic and copies ran while one was open for 16% -> 13% of each run, Pallas kernels for 18% -> 18%
where the time goes in v1:
time: 536 us; the launch traced here: 526 us
  starting transfers between devices  157 us (29%)
  waiting for transfers between devices  151 us (28%)
  Pallas kernels  129 us (24%)
  other arithmetic  57.6 us (11%)
  local copies, waits for them, and re-layouts  16.2 us (3%)
  between operations  11.6 us (2%)
    ppermute x69, starting transfers between devices, moved(): return lax.ppermute(block, ('dp', 'section'), pairs)  157 us
    ppermute x69, waiting for transfers between devices, moved(): return lax.ppermute(block, ('dp', 'section'), pairs)  151 us
    pallas_call x10, Pallas kernels, backward_call(): pl.pallas_call(functools.partial(backward_body, heads, fresh), out_shape=...  55.2 us
    pallas_call x10, Pallas kernels, forward_call(): pl.pallas_call(functools.partial(forward_body, heads, slides, shrink, fre...  52.8 us
    pallas_call x1, Pallas kernels, weight_grads(): pl.pallas_call(functools.partial(weight_grads_body, (rows, micro, tok)),...  13 us
    sub x5, other arithmetic, adam(): weight - rate * (mhat / (jnp.sqrt(vhat) + ADAM_EPS) + decay * weight)  12.5 us
  transfers between devices with their start and end apart: 69, of which 28 were waited for; matrix products, arithmetic and copies ran while one was open for 13% of the time, Pallas kernels for 18%

profile of v1, /device:TPU:0, one launch (start us, length us, event | category | flops | bytes accessed | tf_op | source)
XLA Modules:
  0.0 526.3 jit_solution(16911812887614115762)
XLA Ops:
  21.3 5.4 %multiply_sine_fusion.1 = (f32[4,128,192]{2,1,0:T(8,128)}, f32[4,128,192]{2,1,0:T(8,128)}, f32[4,128,192]{2,1,0:T(8,128)}, f32[4,128,192]{2,1,0:T(8,128)}) fusion(f32[192]{0:T(256)S(1)} %multiply_exponential_fusion, f32[4,128]{1,0:T(4,128)S(1)} %get-tuple-element.635, f32[4,128]{1,0:T(4,128)S(1)} %get-tuple-element.636), kind=kLoop, calls=%fused_computation.54 | loop fusion | flops 196608 | bytes 1577728 | tf_op jit(solution)/shard_map/vmap()/sin | solution.py:64
  26.7 6.4 %collective-permute-done.9 = bf16[1,416,768]{2,1,0:T(8,128)(2,1)} collective-permute-done((bf16[1,416,768]{2,1,0:T(8,128)(2,1)S(1)}, bf16[1,416,768]{2,1,0:T(8,128)(2,1)}, u32[]{:S(2)}, u32[]{:S(2)}) %collective-permute-start.9) | collective-permute-done | bytes 639008 | tf_op jit(solution)/shard_map/ppermute | solution.py:32
  35.5 18.4 %collective-permute-done.2.refs_2_ = bf16[2,3,48,3072]{3,2,1,0:T(8,128)(2,1)} collective-permute-done((bf16[2,3,48,3072]{3,2,1,0:T(8,128)(2,1)}, bf16[2,3,48,3072]{3,2,1,0:T(8,128)(2,1)}, u32[]{:S(2)}, u32[]{:S(2)}) %collective-permute-start.2) | collective-permute-done | bytes 1769504 | tf_op jit(solution)/shard_map/ppermute | solution.py:32
  72.3 11.1 %collective-permute-done.5.refs_3_ = bf16[3,48,3072]{2,1,0:T(8,128)(2,1)} collective-permute-done((bf16[3,48,3072]{2,1,0:T(8,128)(2,1)}, bf16[3,48,3072]{2,1,0:T(8,128)(2,1)}, u32[]{:S(2)}, u32[]{:S(2)}) %collective-permute-start.5) | collective-permute-done | bytes 884768 | tf_op jit(solution)/shard_map/ppermute | solution.py:32
  96.8 9.1 %collective-permute-start.17 = (bf16[3,48,3072]{2,1,0:T(8,128)(2,1)}, bf16[3,48,3072]{2,1,0:T(8,128)(2,1)}, u32[]{:S(2)}, u32[]{:S(2)}) collective-permute-start(bf16[3,48,3072]{2,1,0:T(8,128)(2,1)} %collective-permute-done.5.refs_3_), channel_id=1, source_target_pairs={{0,1},{3,2},{4,5},{7,6},{8,9},{11,10},{12,13},{15,14},{17,16},{18,... | collective-permute-start | bytes 2654216 | tf_op jit(solution)/shard_map/ppermute | solution.py:32
  111.5 7.2 %collective-permute-start.11 = (s32[2,236]{1,0:T(2,128)S(1)}, s32[2,236]{1,0:T(2,128)S(1)}, u32[]{:S(2)}, u32[]{:S(2)}) collective-permute-start(s32[2,236]{1,0:T(2,128)S(1)} %fusion.22), channel_id=1, source_target_pairs={{0,16},{1,17},{2,18},{3,19},{4,20},{5,21},{6,22},{7,23},{8,24},{9,... | collective-permute-start | bytes 5672 | tf_op jit(solution)/shard_map/ppermute | solution.py:32
  125.7 8.2 %load_weights.1 = (bf16[768,2304]{1,0:T(8,128)(2,1)S(1)}, bf16[768,768]{1,0:T(8,128)(2,1)S(1)}, bf16[768,3072]{1,0:T(8,128)(2,1)S(1)}, bf16[768,3072]{1,0:T(8,12...) custom-call(s32[17]{0:T(128)S(1)} %stack.437.scal, ...), custom_call_target="tpu_custom_call" | custom-call | tf_op jit(solution)/shard_map/load_weights/pallas_call | solution.py:443
  133.9 8.6 %layer_forward.10 = (bf16[128,768]{1,0:T(8,128)(2,1)S(1)}, bf16[4,128,768]{2,1,0:T(8,128)(2,1)}, bf16[4,128,2304]{2,1,0:T(8,128)(2,1)}, f32[4,16,128]{2,1,0:T(8,...) custom-call(s32[4]{0:T(128)S(1)} %get-tuple-element.652.refs_0_, ...), custom_call_target="tpu_custom_call" | custom-call | flops 7516192768 | bytes 8388608 | tf_op jit(solution)/shard_map/layer_forward/pallas_call | solution.py:537
  145.7 7.9 %layer_forward.11 = (bf16[128,768]{1,0:T(8,128)(2,1)S(1)}, bf16[4,128,768]{2,1,0:T(8,128)(2,1)}, bf16[4,128,2304]{2,1,0:T(8,128)(2,1)}, f32[4,16,128]{2,1,0:T(8,...) custom-call(s32[4]{0:T(128)S(1)} %get-tuple-element.651.refs_0_, ...), custom_call_target="tpu_custom_call", output_to_operand_aliasing={{1}: (18, {}), {2}: (19, {}), {3}: (20, {}), {4}: (21, {}),... | custom-call | flops 7516192768 | bytes 8388608 | tf_op jit(solution)/shard_map/layer_forward/pallas_call | solution.py:537
  154.9 7.9 %layer_forward.12 = (bf16[128,768]{1,0:T(8,128)(2,1)S(1)}, bf16[4,128,768]{2,1,0:T(8,128)(2,1)}, bf16[4,128,2304]{2,1,0:T(8,128)(2,1)}, f32[4,16,128]{2,1,0:T(8,...) custom-call(s32[4]{0:T(128)S(1)} %add_add_fusion.6.refs_0_, ...), custom_call_target="tpu_custom_call", output_to_operand_aliasing={{1}: (18, {}), {2}: (19, {}), {3}: (20, {}), {4}: (21, {}),... | custom-call | flops 7516192768 | bytes 8388608 | tf_op jit(solution)/shard_map/layer_forward/pallas_call | solution.py:537
  164.1 8.2 %layer_forward.13 = (bf16[128,768]{1,0:T(8,128)(2,1)S(1)}, bf16[4,128,768]{2,1,0:T(8,128)(2,1)}, bf16[4,128,2304]{2,1,0:T(8,128)(2,1)}, f32[4,16,128]{2,1,0:T(8,...) custom-call(s32[4]{0:T(128)S(1)} %add_add_fusion.5.refs_0_, ...), custom_call_target="tpu_custom_call", output_to_operand_aliasing={{1}: (18, {}), {2}: (19, {}), {3}: (20, {}), {4}: (21, {}),... | custom-call | flops 7516192768 | bytes 8388608 | tf_op jit(solution)/shard_map/layer_forward/pallas_call | solution.py:537
  177.6 11.7 %collective-permute-start.29 = (bf16[128,768]{1,0:T(8,128)(2,1)S(1)}, bf16[128,768]{1,0:T(8,128)(2,1)S(1)}, u32[]{:S(2)}, u32[]{:S(2)}) collective-permute-start(bf16[128,768]{1,0:T(8,128)(2,1)S(1)} %get-tuple-element.440), channel_id=1, source_target_pairs={{0,16},{1,17},{4,20},{5,21},{8,24},{9,25},{12,28},{13,29},{16,18},... | collective-permute-start | bytes 589832 | tf_op jit(solution)/shard_map/ppermute | solution.py:32
  190.1 10.6 %collective-permute-start.28 = (bf16[128,768]{1,0:T(8,128)(2,1)S(1)}, bf16[128,768]{1,0:T(8,128)(2,1)S(1)}, u32[]{:S(2)}, u32[]{:S(2)}) collective-permute-start(bf16[128,768]{1,0:T(8,128)(2,1)S(1)} %get-tuple-element.439), channel_id=1, source_target_pairs={{0,16},{1,17},{4,20},{5,21},{8,24},{9,25},{12,28},{13,29},{16,18},... | collective-permute-start | bytes 589832 | tf_op jit(solution)/shard_map/ppermute | solution.py:32
  200.7 7.6 %layer_forward.16 = (bf16[128,768]{1,0:T(8,128)(2,1)S(1)}, bf16[4,128,768]{2,1,0:T(8,128)(2,1)}, bf16[4,128,2304]{2,1,0:T(8,128)(2,1)}, f32[4,16,128]{2,1,0:T(8,...) custom-call(s32[4]{0:T(128)S(1)} %add_add_fusion.8.refs_0_, ...), custom_call_target="tpu_custom_call", output_to_operand_aliasing={{1}: (18, {}), {2}: (19, {}), {3}: (20, {}), {4}: (21, {}),... | custom-call | flops 7516192768 | bytes 8388608 | tf_op jit(solution)/shard_map/layer_forward/pallas_call | solution.py:537
  218.3 9.2 %layer_forward.19 = (bf16[128,768]{1,0:T(8,128)(2,1)}, bf16[4,128,768]{2,1,0:T(8,128)(2,1)}, bf16[4,128,2304]{2,1,0:T(8,128)(2,1)}, f32[4,16,128]{2,1,0:T(8,128)...) custom-call(s32[4]{0:T(128)S(1)} %add_add_fusion.refs_0_, ...), custom_call_target="tpu_custom_call", output_to_operand_aliasing={{1}: (18, {}), {2}: (19, {}), {3}: (20, {}), {4}: (21, {}),... | custom-call | flops 7516192768 | bytes 8388608 | tf_op jit(solution)/shard_map/layer_forward/pallas_call | solution.py:537
  231.3 19.4 %collective-permute-done.33.refs_3_ = bf16[128,768]{1,0:T(8,128)(2,1)S(1)} collective-permute-done((bf16[128,768]{1,0:T(8,128)(2,1)S(1)}, bf16[128,768]{1,0:T(8,128)(2,1)S(1)}, u32[]{:S(2)}, u32[]{:S(2)}) %collective-permute-start.33) | collective-permute-done | bytes 196640 | tf_op jit(solution)/shard_map/ppermute | solution.py:32
  250.8 8.3 %layer_backward.12 = (bf16[128,768]{1,0:T(8,128)(2,1)S(1)}, bf16[4,128,768]{2,1,0:T(8,128)(2,1)S(1)}, bf16[4,128,3072]{2,1,0:T(8,128)(2,1)S(1)}, bf16[4,128,768]...) custom-call(s32[4]{0:T(128)S(1)} %add_add_fusion.16.refs_0_, ...), custom_call_target="tpu_custom_call", output_to_operand_aliasing={{1}: (15, {}), {2}: (16, {}), {3}: (17, {}), {4}: (18, {}),... | custom-call | flops 10737418240 | bytes 8388608 | tf_op jit(solution)/shard_map/layer_backward/pallas_call | solution.py:571
  262.3 8.1 %collective-permute-done.35.refs_3_ = bf16[128,768]{1,0:T(8,128)(2,1)S(1)} collective-permute-done((bf16[128,768]{1,0:T(8,128)(2,1)S(1)}, bf16[128,768]{1,0:T(8,128)(2,1)S(1)}, u32[]{:S(2)}, u32[]{:S(2)}) %collective-permute-start.35) | collective-permute-done | bytes 196640 | tf_op jit(solution)/shard_map/ppermute | solution.py:32
  272.4 8.5 %layer_backward.15 = (bf16[128,768]{1,0:T(8,128)(2,1)S(1)}, bf16[4,128,768]{2,1,0:T(8,128)(2,1)S(1)}, bf16[4,128,3072]{2,1,0:T(8,128)(2,1)S(1)}, bf16[4,128,768]...) custom-call(s32[4]{0:T(128)S(1)} %add_add_fusion.12.refs_0_, ...), custom_call_target="tpu_custom_call", output_to_operand_aliasing={{1}: (15, {}), {2}: (16, {}), {3}: (17, {}), {4}: (18, {}),... | custom-call | flops 10737418240 | bytes 8388608 | tf_op jit(solution)/shard_map/layer_backward/pallas_call | solution.py:571
  286.4 8.8 %layer_backward.16 = (bf16[128,768]{1,0:T(8,128)(2,1)S(1)}, bf16[4,128,768]{2,1,0:T(8,128)(2,1)S(1)}, bf16[4,128,3072]{2,1,0:T(8,128)(2,1)S(1)}, bf16[4,128,768]...) custom-call(s32[4]{0:T(128)S(1)} %add_add_fusion.18.refs_0_, ...), custom_call_target="tpu_custom_call", output_to_operand_aliasing={{1}: (15, {}), {2}: (16, {}), {3}: (17, {}), {4}: (18, {}),... | custom-call | flops 10737418240 | bytes 8388608 | tf_op jit(solution)/shard_map/layer_backward/pallas_call | solution.py:571
  297.3 8.8 %layer_backward.17 = (bf16[128,768]{1,0:T(8,128)(2,1)S(1)}, bf16[4,128,768]{2,1,0:T(8,128)(2,1)S(1)}, bf16[4,128,3072]{2,1,0:T(8,128)(2,1)S(1)}, bf16[4,128,768]...) custom-call(s32[4]{0:T(128)S(1)} %add_add_fusion.11.refs_0_, ...), custom_call_target="tpu_custom_call", output_to_operand_aliasing={{1}: (15, {}), {2}: (16, {}), {3}: (17, {}), {4}: (18, {}),... | custom-call | flops 10737418240 | bytes 8388608 | tf_op jit(solution)/shard_map/layer_backward/pallas_call | solution.py:571
  308.1 9.1 %layer_backward.18 = (bf16[128,768]{1,0:T(8,128)(2,1)S(1)}, bf16[4,128,768]{2,1,0:T(8,128)(2,1)S(1)}, bf16[4,128,3072]{2,1,0:T(8,128)(2,1)S(1)}, bf16[4,128,768]...) custom-call(s32[4]{0:T(128)S(1)} %add_add_fusion.19.refs_0_, ...), custom_call_target="tpu_custom_call", output_to_operand_aliasing={{1}: (15, {}), {2}: (16, {}), {3}: (17, {}), {4}: (18, {}),... | custom-call | flops 10737418240 | bytes 8388608 | tf_op jit(solution)/shard_map/layer_backward/pallas_call | solution.py:571
  317.2 9.3 %layer_backward.19 = (bf16[128,768]{1,0:T(8,128)(2,1)S(1)}, bf16[4,128,768]{2,1,0:T(8,128)(2,1)S(1)}, bf16[4,128,3072]{2,1,0:T(8,128)(2,1)S(1)}, bf16[4,128,768]...) custom-call(s32[4]{0:T(128)S(1)} %add_add_fusion.10.refs_0_, ...), custom_call_target="tpu_custom_call", output_to_operand_aliasing={{1}: (15, {}), {2}: (16, {}), {3}: (17, {}), {4}: (18, {}),... | custom-call | flops 10737418240 | bytes 8388608 | tf_op jit(solution)/shard_map/layer_backward/pallas_call | solution.py:571
  326.5 13.0 %weight_grads.1 = (bf16[3,96,3072]{2,1,0:T(8,128)(2,1)}, bf16[3,288,3072]{2,1,0:T(8,128)(2,1)}, bf16[3,384,3072]{2,1,0:T(8,128)(2,1)}) custom-call(s32[8]{0:T(128)S(1)} %stack.405.order, bf16[4,128,768]{2,1,0:T(8,128)(2,1)} %get-tuple-element.495.refs_0_, bf16[4,128,768]{2,1,0:T(8,128)(2,1)} %get-tuple-element.496.refs_1_, ...), custom_call_target="tpu_custom_call" | custom-call | flops 7247757312 | bytes 28311552 | tf_op jit(solution)/shard_map/weight_grads/pallas_call | solution.py:501
  352.7 19.7 %collective-permute-done.48 = bf16[128,768]{1,0:T(8,128)(2,1)S(1)} collective-permute-done((bf16[128,768]{1,0:T(8,128)(2,1)S(1)}, bf16[128,768]{1,0:T(8,128)(2,1)S(1)}, u32[]{:S(2)}, u32[]{:S(2)}) %collective-permute-start.48) | collective-permute-done | bytes 196640 | tf_op jit(solution)/shard_map/ppermute | solution.py:32
  377.5 5.4 %fusion.2 = (bf16[3,96,3072]{2,1,0:T(8,128)(2,1)}, bf16[3,96,3072]{2,1,0:T(8,128)(2,1)}) fusion(bf16[3,3,96,3072]{3,2,1,0:T(8,128)(2,1)} %bitcast.88, bf16[3,4,96,3072]{3,2,1,0:T(8,128)(2,1)} %bitcast.219, bf16[3,48,3072]{2,1,0:T(8,128)(2,1)} %collective-permute-done.42, bf16[3,48,3072]{2,1,0:T(8,128)(2,1)} %collective-permute-done.43), kind=kLoop, calls=%fused_computation.5 | loop fusion | flops 10616832 | bytes 12386304 | tf_op jit(solution)/shard_map/convert_element_type | solution.py:797
  391.9 9.5 %collective-permute-done.51 = f32[24,768]{1,0:T(8,128)S(1)} collective-permute-done((f32[24,768]{1,0:T(8,128)S(1)}, f32[24,768]{1,0:T(8,128)S(1)}, u32[]{:S(2)}, u32[]{:S(2)}) %collective-permute-start.51) | collective-permute-done | bytes 73760 | tf_op jit(solution)/shard_map/ppermute | solution.py:32
  402.2 5.5 %fusion.5 = bf16[3,96,3072]{2,1,0:T(8,128)(2,1)} fusion(bf16[3,96,3072]{2,1,0:T(8,128)(2,1)} %collective-permute-done.45, bf16[3,96,3072]{2,1,0:T(8,128)(2,1)} %collective-permute-done.44, bf16[3,4,96,3072]{3,2,1,0:T(8,128)(2,1)} %bitcast.220, bf16[3,3,96,3072]{3,2,1,0:T(8,128)(2,1)} %bitcast.88), kind=kLoop, calls=%fused_computation.11 | loop fusion | flops 7077888 | bytes 8847360 | tf_op jit(solution)/shard_map/convert_element_type | solution.py:803
  419.4 13.7 %collective-permute-done.54 = bf16[3,96,3072]{2,1,0:T(8,128)(2,1)} collective-permute-done((bf16[3,96,3072]{2,1,0:T(8,128)(2,1)}, bf16[3,96,3072]{2,1,0:T(8,128)(2,1)}, u32[]{:S(2)}, u32[]{:S(2)}) %collective-permute-start.54) | collective-permute-done | bytes 1769504 | tf_op jit(solution)/shard_map/ppermute | solution.py:32
  457.9 13.7 %collective-permute-start.61 = (f32[2,768]{1,0:T(2,128)S(1)}, f32[2,768]{1,0:T(2,128)S(1)}, u32[]{:S(2)}, u32[]{:S(2)}) collective-permute-start(f32[2,768]{1,0:T(2,128)S(1)} %slice.140), channel_id=1, source_target_pairs={{0,16},{1,17},{2,18},{3,19},{4,20},{5,21},{6,22},{7,23},{8,24},{9,... | collective-permute-start | bytes 18440 | tf_op jit(solution)/shard_map/ppermute | solution.py:32
  476.7 6.0 %collective-permute-done.60 = f32[20,768]{1,0:T(8,128)S(1)} collective-permute-done((f32[20,768]{1,0:T(8,128)S(1)}, f32[20,768]{1,0:T(8,128)S(1)}, u32[]{:S(2)}, u32[]{:S(2)}) %collective-permute-start.60) | collective-permute-done | bytes 61472 | tf_op jit(solution)/shard_map/ppermute | solution.py:32
  506.1 8.3 %multiply_subtract_fusion = (f32[1,3,96,3072]{3,2,1,0:T(8,128)}, f32[1,3,96,3072]{3,2,1,0:T(8,128)}, f32[1,3,96,3072]{3,2,1,0:T(8,128)}) fusion(f32[1,3,96,3072]{3,2,1,0:T(8,128)} %param.25, f32[]{:T(128)S(6)} %mul.468, bf16[3,96,3072]{2,1,0:T(8,128)(2,1)S(1)} %fusion.7, bf16[3,96,3072]{2,1,0:T(8,128)(2,1)} %collective-permute-done.53, pred[]{:T(512)S(6)} %eq.206, ...), kind=kLoop, calls=%fused_computation.14 | loop fusion | flops 15925248 | bytes 24772612 | tf_op jit(solution)/shard_map/sub | solution.py:614
  (322 shorter events, 202.3 us)
Async XLA Ops:
  4.4 31.1 %collective-permute-start = (bf16[2,3,48,3072]{3,2,1,0:T(8,128)(2,1)}, bf16[2,3,48,3072]{3,2,1,0:T(8,128)(2,1)}, u32[]{:S(2)}, u32[]{:S(2)}) collective-permute-start(bf16[2,3,48,3072]{3,2,1,0:T(8,128)(2,1)} %bitcast.213.refs_0_), channel_id=1, source_target_pairs={{1,16},{2,19},{5,20},{6,23},{9,24},{10,27},{13,28},{14,31},{16,1},... | collective-permute-start | bytes 5308424 | tf_op jit(solution)/shard_map/ppermute | solution.py:32
  6.5 29.0 %collective-permute-start.1 = (bf16[2,3,48,3072]{3,2,1,0:T(8,128)(2,1)}, bf16[2,3,48,3072]{3,2,1,0:T(8,128)(2,1)}, u32[]{:S(2)}, u32[]{:S(2)}) collective-permute-start(bf16[2,3,48,3072]{3,2,1,0:T(8,128)(2,1)} %bitcast.213.refs_0_), channel_id=1, source_target_pairs={{0,4},{3,7},{4,0},{7,3},{8,12},{11,15},{12,8},{15,11},{17,21},{18,... | collective-permute-start | bytes 5308424 | tf_op jit(solution)/shard_map/ppermute | solution.py:32
  11.3 42.6 %collective-permute-start.2 = (bf16[2,3,48,3072]{3,2,1,0:T(8,128)(2,1)}, bf16[2,3,48,3072]{3,2,1,0:T(8,128)(2,1)}, u32[]{:S(2)}, u32[]{:S(2)}) collective-permute-start(bf16[2,3,48,3072]{3,2,1,0:T(8,128)(2,1)} %bitcast.213.refs_0_), channel_id=1, source_target_pairs={{0,8},{3,11},{4,12},{7,15},{8,0},{11,3},{12,4},{15,7},{17,25},{18,... | collective-permute-start | bytes 5308424 | tf_op jit(solution)/shard_map/ppermute | solution.py:32
  14.8 50.5 %collective-permute-start.7 = (bf16[2,3,48,3072]{3,2,1,0:T(8,128)(2,1)}, bf16[2,3,48,3072]{3,2,1,0:T(8,128)(2,1)}, u32[]{:S(2)}, u32[]{:S(2)}) collective-permute-start(bf16[2,3,48,3072]{3,2,1,0:T(8,128)(2,1)} %bitcast.213.refs_0_), channel_id=1, source_target_pairs={{0,1},{3,2},{4,5},{7,6},{8,9},{11,10},{12,13},{15,14},{17,16},{18,... | collective-permute-start | bytes 5308424 | tf_op jit(solution)/shard_map/ppermute | solution.py:32
  34.3 29.0 %collective-permute-start.10 = (bf16[2,1,416,768]{3,2,1,0:T(8,128)(2,1)S(1)}, bf16[2,1,416,768]{3,2,1,0:T(8,128)(2,1)S(1)}, u32[]{:S(2)}, u32[]{:S(2)}) collective-permute-start(bf16[2,1,416,768]{3,2,1,0:T(8,128)(2,1)S(1)} %pad_maximum_fusion), channel_id=1, source_target_pairs={{0,1},{1,0},{2,3},{3,2},{4,5},{5,4},{6,7},{7,6},{8,9},{9,8},{10,11... | collective-permute-start | bytes 3833864 | tf_op jit(solution)/shard_map/ppermute | solution.py:32
  53.9 34.4 %collective-permute-start.3 = (bf16[2,3,48,3072]{3,2,1,0:T(8,128)(2,1)}, bf16[2,3,48,3072]{3,2,1,0:T(8,128)(2,1)}, u32[]{:S(2)}, u32[]{:S(2)}) collective-permute-start(bf16[2,3,48,3072]{3,2,1,0:T(8,128)(2,1)} %collective-permute-done.refs_10_), channel_id=1, source_target_pairs={{1,5},{2,6},{5,1},{6,2},{9,13},{10,14},{13,9},{14,10},{16,20},{19,... | collective-permute-start | bytes 5308424 | tf_op jit(solution)/shard_map/ppermute | solution.py:32
  55.8 32.6 %collective-permute-start.4 = (bf16[2,3,48,3072]{3,2,1,0:T(8,128)(2,1)}, bf16[2,3,48,3072]{3,2,1,0:T(8,128)(2,1)}, u32[]{:S(2)}, u32[]{:S(2)}) collective-permute-start(bf16[2,3,48,3072]{3,2,1,0:T(8,128)(2,1)} %collective-permute-done.refs_10_), channel_id=1, source_target_pairs={{1,9},{2,10},{5,13},{6,14},{9,1},{10,2},{13,5},{14,6},{16,24},{19,... | collective-permute-start | bytes 5308424 | tf_op jit(solution)/shard_map/ppermute | solution.py:32
  57.7 30.7 %collective-permute-start.8 = (bf16[2,3,48,3072]{3,2,1,0:T(8,128)(2,1)}, bf16[2,3,48,3072]{3,2,1,0:T(8,128)(2,1)}, u32[]{:S(2)}, u32[]{:S(2)}) collective-permute-start(bf16[2,3,48,3072]{3,2,1,0:T(8,128)(2,1)} %collective-permute-done.refs_10_), channel_id=1, source_target_pairs={{1,0},{2,3},{5,4},{6,7},{9,8},{10,11},{13,12},{14,15},{16,17},{19,... | collective-permute-start | bytes 5308424 | tf_op jit(solution)/shard_map/ppermute | solution.py:32
  63.2 20.1 %collective-permute-start.5 = (bf16[3,48,3072]{2,1,0:T(8,128)(2,1)}, bf16[3,48,3072]{2,1,0:T(8,128)(2,1)}, u32[]{:S(2)}, u32[]{:S(2)}) collective-permute-start(bf16[3,48,3072]{2,1,0:T(8,128)(2,1)} %slice_bitcast_fusion.11), channel_id=1, source_target_pairs={{0,4},{3,7},{4,0},{7,3},{8,12},{11,15},{12,8},{15,11},{17,21},{18,... | collective-permute-start | bytes 2654216 | tf_op jit(solution)/shard_map/ppermute | solution.py:32
  65.3 21.2 %collective-permute-start.6 = (bf16[3,48,3072]{2,1,0:T(8,128)(2,1)}, bf16[3,48,3072]{2,1,0:T(8,128)(2,1)}, u32[]{:S(2)}, u32[]{:S(2)}) collective-permute-start(bf16[3,48,3072]{2,1,0:T(8,128)(2,1)} %slice_bitcast_fusion.10), channel_id=1, source_target_pairs={{0,8},{3,11},{4,12},{7,15},{8,0},{11,3},{12,4},{15,7},{17,25},{18,... | collective-permute-start | bytes 2654216 | tf_op jit(solution)/shard_map/ppermute | solution.py:32
  89.6 29.1 %collective-permute-start.20 = (bf16[2,3,48,3072]{3,2,1,0:T(8,128)(2,1)}, bf16[2,3,48,3072]{3,2,1,0:T(8,128)(2,1)}, u32[]{:S(2)}, u32[]{:S(2)}) collective-permute-start(bf16[2,3,48,3072]{3,2,1,0:T(8,128)(2,1)} %collective-permute-done.4.refs_12_), channel_id=1, source_target_pairs={{1,0},{2,3},{5,4},{6,7},{9,8},{10,11},{13,12},{14,15},{16,17},{19,... | collective-permute-start | bytes 5308424 | tf_op jit(solution)/shard_map/ppermute | solution.py:32
  91.7 27.1 %collective-permute-start.19 = (bf16[2,3,48,3072]{3,2,1,0:T(8,128)(2,1)}, bf16[2,3,48,3072]{3,2,1,0:T(8,128)(2,1)}, u32[]{:S(2)}, u32[]{:S(2)}) collective-permute-start(bf16[2,3,48,3072]{3,2,1,0:T(8,128)(2,1)} %collective-permute-done.3.refs_11_), channel_id=1, source_target_pairs={{1,0},{2,3},{5,4},{6,7},{9,8},{10,11},{13,12},{14,15},{16,17},{19,... | collective-permute-start | bytes 5308424 | tf_op jit(solution)/shard_map/ppermute | solution.py:32
  95.1 16.4 %collective-permute-start.14 = (bf16[3,48,3072]{2,1,0:T(8,128)(2,1)}, bf16[3,48,3072]{2,1,0:T(8,128)(2,1)}, u32[]{:S(2)}, u32[]{:S(2)}) collective-permute-start(bf16[3,48,3072]{2,1,0:T(8,128)(2,1)} %slice_bitcast_fusion.8), channel_id=1, source_target_pairs={{1,9},{2,10},{5,13},{6,14},{9,1},{10,2},{13,5},{14,6},{16,24},{19,... | collective-permute-start | bytes 2654216 | tf_op jit(solution)/shard_map/ppermute | solution.py:32
  96.8 22.0 %collective-permute-start.17 = (bf16[3,48,3072]{2,1,0:T(8,128)(2,1)}, bf16[3,48,3072]{2,1,0:T(8,128)(2,1)}, u32[]{:S(2)}, u32[]{:S(2)}) collective-permute-start(bf16[3,48,3072]{2,1,0:T(8,128)(2,1)} %collective-permute-done.5.refs_3_), channel_id=1, source_target_pairs={{0,1},{3,2},{4,5},{7,6},{8,9},{11,10},{12,13},{15,14},{17,16},{18,... | collective-permute-start | bytes 2654216 | tf_op jit(solution)/shard_map/ppermute | solution.py:32
  122.6 32.2 %collective-permute-start.23 = (bf16[2,128,768]{2,1,0:T(8,128)(2,1)S(1)}, bf16[2,128,768]{2,1,0:T(8,128)(2,1)S(1)}, u32[]{:S(2)}, u32[]{:S(2)}) collective-permute-start(bf16[2,128,768]{2,1,0:T(8,128)(2,1)S(1)} %constant_dynamic-slice_fusion.3), channel_id=1, source_target_pairs={{16,0},{17,1},{20,4},{21,5},{24,8},{25,9},{28,12},{29,13}} | collective-permute-start | bytes 1179656 | tf_op jit(solution)/shard_map/ppermute | solution.py:32
  172.3 17.0 %collective-permute-start.26 = (bf16[128,768]{1,0:T(8,128)(2,1)S(1)}, bf16[128,768]{1,0:T(8,128)(2,1)S(1)}, u32[]{:S(2)}, u32[]{:S(2)}) collective-permute-start(bf16[128,768]{1,0:T(8,128)(2,1)S(1)} %get-tuple-element.411), channel_id=1, source_target_pairs={{0,16},{1,17},{4,20},{5,21},{8,24},{9,25},{12,28},{13,29},{16,18},... | collective-permute-start | bytes 589832 | tf_op jit(solution)/shard_map/ppermute | solution.py:32
  177.6 23.1 %collective-permute-start.29 = (bf16[128,768]{1,0:T(8,128)(2,1)S(1)}, bf16[128,768]{1,0:T(8,128)(2,1)S(1)}, u32[]{:S(2)}, u32[]{:S(2)}) collective-permute-start(bf16[128,768]{1,0:T(8,128)(2,1)S(1)} %get-tuple-element.440), channel_id=1, source_target_pairs={{0,16},{1,17},{4,20},{5,21},{8,24},{9,25},{12,28},{13,29},{16,18},... | collective-permute-start | bytes 589832 | tf_op jit(solution)/shard_map/ppermute | solution.py:32
  190.1 20.1 %collective-permute-start.28 = (bf16[128,768]{1,0:T(8,128)(2,1)S(1)}, bf16[128,768]{1,0:T(8,128)(2,1)S(1)}, u32[]{:S(2)}, u32[]{:S(2)}) collective-permute-start(bf16[128,768]{1,0:T(8,128)(2,1)S(1)} %get-tuple-element.439), channel_id=1, source_target_pairs={{0,16},{1,17},{4,20},{5,21},{8,24},{9,25},{12,28},{13,29},{16,18},... | collective-permute-start | bytes 589832 | tf_op jit(solution)/shard_map/ppermute | solution.py:32
  228.1 22.7 %collective-permute-start.33 = (bf16[128,768]{1,0:T(8,128)(2,1)S(1)}, bf16[128,768]{1,0:T(8,128)(2,1)S(1)}, u32[]{:S(2)}, u32[]{:S(2)}) collective-permute-start(bf16[128,768]{1,0:T(8,128)(2,1)S(1)} %get-tuple-element.510), channel_id=1, source_target_pairs={{2,18},{3,19},{6,22},{7,23},{10,26},{11,27},{14,30},{15,31},{16,0}... | collective-permute-start | bytes 589832 | tf_op jit(solution)/shard_map/ppermute | solution.py:32
  230.0 30.3 %collective-permute-start.32 = (bf16[128,768]{1,0:T(8,128)(2,1)S(1)}, bf16[128,768]{1,0:T(8,128)(2,1)S(1)}, u32[]{:S(2)}, u32[]{:S(2)}) collective-permute-start(bf16[128,768]{1,0:T(8,128)(2,1)S(1)} %get-tuple-element.509), channel_id=1, source_target_pairs={{2,18},{3,19},{6,22},{7,23},{10,26},{11,27},{14,30},{15,31},{16,0}... | collective-permute-start | bytes 589832 | tf_op jit(solution)/shard_map/ppermute | solution.py:32
  343.5 34.0 %collective-permute-start.41 = (bf16[3,288,3072]{2,1,0:T(8,128)(2,1)}, bf16[3,288,3072]{2,1,0:T(8,128)(2,1)}, u32[]{:S(2)}, u32[]{:S(2)}) collective-permute-start(bf16[3,288,3072]{2,1,0:T(8,128)(2,1)} %get-tuple-element.565), channel_id=1, source_target_pairs={{0,1},{1,0},{2,3},{3,2},{4,5},{5,4},{6,7},{7,6},{8,9},{9,8},{10,11... | collective-permute-start | bytes 15925256 | tf_op jit(solution)/shard_map/ppermute | solution.py:32
  347.0 30.5 %collective-permute-start.42 = (bf16[3,48,3072]{2,1,0:T(8,128)(2,1)}, bf16[3,48,3072]{2,1,0:T(8,128)(2,1)}, u32[]{:S(2)}, u32[]{:S(2)}) collective-permute-start(bf16[3,48,3072]{2,1,0:T(8,128)(2,1)} %get-tuple-element.566), channel_id=1, source_target_pairs={{0,4},{1,5},{2,6},{3,7},{4,0},{5,1},{6,2},{7,3},{8,12},{9,13},{10,... | collective-permute-start | bytes 2654216 | tf_op jit(solution)/shard_map/ppermute | solution.py:32
  348.0 29.5 %collective-permute-start.43 = (bf16[3,48,3072]{2,1,0:T(8,128)(2,1)}, bf16[3,48,3072]{2,1,0:T(8,128)(2,1)}, u32[]{:S(2)}, u32[]{:S(2)}) collective-permute-start(bf16[3,48,3072]{2,1,0:T(8,128)(2,1)} %get-tuple-element.567), channel_id=1, source_target_pairs={{0,8},{1,9},{2,10},{3,11},{4,12},{5,13},{6,14},{7,15},{8,0},{9,1},... | collective-permute-start | bytes 2654216 | tf_op jit(solution)/shard_map/ppermute | solution.py:32
  348.0 24.4 %collective-permute-start.48 = (bf16[128,768]{1,0:T(8,128)(2,1)S(1)}, bf16[128,768]{1,0:T(8,128)(2,1)S(1)}, u32[]{:S(2)}, u32[]{:S(2)}) collective-permute-start(bf16[128,768]{1,0:T(8,128)(2,1)S(1)} %get-tuple-element.575), channel_id=1, source_target_pairs={{0,16},{1,17},{4,20},{5,21},{8,24},{9,25},{12,28},{13,29}} | collective-permute-start | bytes 589832 | tf_op jit(solution)/shard_map/ppermute | solution.py:32
  350.1 25.9 %collective-permute-start.47 = (bf16[128,768]{1,0:T(8,128)(2,1)S(1)}, bf16[128,768]{1,0:T(8,128)(2,1)S(1)}, u32[]{:S(2)}, u32[]{:S(2)}) collective-permute-start(bf16[128,768]{1,0:T(8,128)(2,1)S(1)} %get-tuple-element.580), channel_id=1, source_target_pairs={{0,16},{1,17},{4,20},{5,21},{8,24},{9,25},{12,28},{13,29}} | collective-permute-start | bytes 589832 | tf_op jit(solution)/shard_map/ppermute | solution.py:32
  382.9 19.3 %collective-permute-start.44 = (bf16[3,96,3072]{2,1,0:T(8,128)(2,1)}, bf16[3,96,3072]{2,1,0:T(8,128)(2,1)}, u32[]{:S(2)}, u32[]{:S(2)}) collective-permute-start(bf16[3,96,3072]{2,1,0:T(8,128)(2,1)} %get-tuple-element.586), channel_id=1, source_target_pairs={{1,5},{2,6},{5,1},{6,2},{9,13},{10,14},{13,9},{14,10},{16,20},{19,... | collective-permute-start | bytes 5308424 | tf_op jit(solution)/shard_map/ppermute | solution.py:32
  384.7 17.5 %collective-permute-start.45 = (bf16[3,96,3072]{2,1,0:T(8,128)(2,1)}, bf16[3,96,3072]{2,1,0:T(8,128)(2,1)}, u32[]{:S(2)}, u32[]{:S(2)}) collective-permute-start(bf16[3,96,3072]{2,1,0:T(8,128)(2,1)} %get-tuple-element.587), channel_id=1, source_target_pairs={{1,9},{2,10},{5,13},{6,14},{9,1},{10,2},{13,5},{14,6},{16,24},{19,... | collective-permute-start | bytes 5308424 | tf_op jit(solution)/shard_map/ppermute | solution.py:32
  407.7 25.3 %collective-permute-start.54 = (bf16[3,96,3072]{2,1,0:T(8,128)(2,1)}, bf16[3,96,3072]{2,1,0:T(8,128)(2,1)}, u32[]{:S(2)}, u32[]{:S(2)}) collective-permute-start(bf16[3,96,3072]{2,1,0:T(8,128)(2,1)} %get-tuple-element.586), channel_id=1, source_target_pairs={{0,4},{3,7},{4,0},{7,3},{8,12},{11,15},{12,8},{15,11},{17,21},{18,... | collective-permute-start | bytes 5308424 | tf_op jit(solution)/shard_map/ppermute | solution.py:32
  410.6 25.0 %collective-permute-start.55 = (bf16[3,96,3072]{2,1,0:T(8,128)(2,1)}, bf16[3,96,3072]{2,1,0:T(8,128)(2,1)}, u32[]{:S(2)}, u32[]{:S(2)}) collective-permute-start(bf16[3,96,3072]{2,1,0:T(8,128)(2,1)} %get-tuple-element.587), channel_id=1, source_target_pairs={{0,8},{3,11},{4,12},{7,15},{8,0},{11,3},{12,4},{15,7},{17,25},{18,... | collective-permute-start | bytes 5308424 | tf_op jit(solution)/shard_map/ppermute | solution.py:32
  414.3 71.4 %collective-permute-start.53 = (bf16[3,96,3072]{2,1,0:T(8,128)(2,1)}, bf16[3,96,3072]{2,1,0:T(8,128)(2,1)}, u32[]{:S(2)}, u32[]{:S(2)}) collective-permute-start(bf16[3,96,3072]{2,1,0:T(8,128)(2,1)} %fusion.5), channel_id=1, source_target_pairs={{1,16},{2,19},{5,20},{6,23},{9,24},{10,27},{13,28},{14,31},{16,1},... | collective-permute-start | bytes 5308424 | tf_op jit(solution)/shard_map/ppermute | solution.py:32
  453.5 20.2 %collective-permute-start.59 = (f32[20,768]{1,0:T(8,128)}, f32[20,768]{1,0:T(8,128)S(1)}, u32[]{:S(2)}, u32[]{:S(2)}) collective-permute-start(f32[20,768]{1,0:T(8,128)} %slice_select_fusion.1), channel_id=1, source_target_pairs={{0,2},{1,3},{2,0},{3,1},{4,6},{5,7},{6,4},{7,5},{8,10},{9,11},{10,... | collective-permute-start | bytes 184328 | tf_op jit(solution)/shard_map/ppermute | solution.py:32
  457.9 18.8 %collective-permute-start.61 = (f32[2,768]{1,0:T(2,128)S(1)}, f32[2,768]{1,0:T(2,128)S(1)}, u32[]{:S(2)}, u32[]{:S(2)}) collective-permute-start(f32[2,768]{1,0:T(2,128)S(1)} %slice.140), channel_id=1, source_target_pairs={{0,16},{1,17},{2,18},{3,19},{4,20},{5,21},{6,22},{7,23},{8,24},{9,... | collective-permute-start | bytes 18440 | tf_op jit(solution)/shard_map/ppermute | solution.py:32
  (71 other events, 981.0 us)

commit v2 on v1

--- a/solution.py
+++ b/solution.py
@@ -203,8 +203,8 @@
             hid_v[:, cols] = act.astype(BF)
             slope = 1.5957691216057308 + 0.21406444881478 * square
             gp_v[:, cols] = sig + act * (1.0 - sig) * slope
-        emit(gp_v, gp_b.at[pick])
-        emit(hid_v, hid_b.at[pick])
+            emit(gp_v.at[:, cols], gp_b.at[pick, :, cols])
+            emit(hid_v.at[:, cols], hid_b.at[pick, :, cols])
         out = mid_v[...] + mm(hid_v[...], w2t[...])
         send_h[...] = out.astype(BF)
 
@@ -548,7 +548,7 @@
             pltpu.VMEM((tok, width), F32),
             pltpu.VMEM((width, tok), BF), pltpu.VMEM((width, tok), BF), pltpu.VMEM((width, tok), F32),
             pltpu.VMEM((rows, width), F32), vm(10), vm(11), vm(12),
-            pltpu.SemaphoreType.DMA((4,)), pltpu.SemaphoreType.DMA((9,)),
+            pltpu.SemaphoreType.DMA((4,)), pltpu.SemaphoreType.DMA((15,)),
         ],
         compiler_params=pltpu.CompilerParams(vmem_limit_bytes=14 << 20),
         cost_estimate=pl.CostEstimate(flops=7 << 30, bytes_accessed=8 << 20, transcendentals=1 << 20),

time: 536 us -> 535 us (level)
  transfers between devices with their start and end apart: 69 -> 69, of which waited for: 28 -> 30; matrix products, arithmetic and copies ran while one was open for 13% -> 13% of each run, Pallas kernels for 18% -> 18%
where the time goes in v2:
time: 535 us; the launch traced here: 525 us
  starting transfers between devices  155 us (29%)
  waiting for transfers between devices  155 us (29%)
  Pallas kernels  125 us (23%)
  other arithmetic  57.6 us (11%)
  local copies, waits for them, and re-layouts  16.2 us (3%)
  between operations  11.6 us (2%)
    ppermute x69, waiting for transfers between devices, moved(): return lax.ppermute(block, ('dp', 'section'), pairs)  155 us
    ppermute x69, starting transfers between devices, moved(): return lax.ppermute(block, ('dp', 'section'), pairs)  155 us
    pallas_call x10, Pallas kernels, backward_call(): pl.pallas_call(functools.partial(backward_body, heads, fresh), out_shape=...  55.2 us
    pallas_call x10, Pallas kernels, forward_call(): pl.pallas_call(functools.partial(forward_body, heads, slides, shrink, fre...  49 us
    pallas_call x1, Pallas kernels, weight_grads(): pl.pallas_call(functools.partial(weight_grads_body, (rows, micro, tok)),...  13 us
    sub x5, other arithmetic, adam(): weight - rate * (mhat / (jnp.sqrt(vhat) + ADAM_EPS) + decay * weight)  12.5 us
  transfers between devices with their start and end apart: 69, of which 30 were waited for; matrix products, arithmetic and copies ran while one was open for 13% of the time, Pallas kernels for 18%

profile of v2, /device:TPU:0, one launch (start us, length us, event | category | flops | bytes accessed | tf_op | source)
XLA Modules:
  0.0 525.4 jit_solution(6380330550529258639)
XLA Ops:
  26.7 6.4 %collective-permute-done.9 = bf16[1,416,768]{2,1,0:T(8,128)(2,1)} collective-permute-done((bf16[1,416,768]{2,1,0:T(8,128)(2,1)S(1)}, bf16[1,416,768]{2,1,0:T(8,128)(2,1)}, u32[]{:S(2)}, u32[]{:S(2)}) %collective-permute-start.9) | collective-permute-done | bytes 639008 | tf_op jit(solution)/shard_map/ppermute | solution.py:32
  35.5 18.4 %collective-permute-done.2.refs_2_ = bf16[2,3,48,3072]{3,2,1,0:T(8,128)(2,1)} collective-permute-done((bf16[2,3,48,3072]{3,2,1,0:T(8,128)(2,1)}, bf16[2,3,48,3072]{3,2,1,0:T(8,128)(2,1)}, u32[]{:S(2)}, u32[]{:S(2)}) %collective-permute-start.2) | collective-permute-done | bytes 1769504 | tf_op jit(solution)/shard_map/ppermute | solution.py:32
  72.3 11.1 %collective-permute-done.5.refs_3_ = bf16[3,48,3072]{2,1,0:T(8,128)(2,1)} collective-permute-done((bf16[3,48,3072]{2,1,0:T(8,128)(2,1)}, bf16[3,48,3072]{2,1,0:T(8,128)(2,1)}, u32[]{:S(2)}, u32[]{:S(2)}) %collective-permute-start.5) | collective-permute-done | bytes 884768 | tf_op jit(solution)/shard_map/ppermute | solution.py:32
  96.8 9.1 %collective-permute-start.17 = (bf16[3,48,3072]{2,1,0:T(8,128)(2,1)}, bf16[3,48,3072]{2,1,0:T(8,128)(2,1)}, u32[]{:S(2)}, u32[]{:S(2)}) collective-permute-start(bf16[3,48,3072]{2,1,0:T(8,128)(2,1)} %collective-permute-done.5.refs_3_), channel_id=1, source_target_pairs={{0,1},{3,2},{4,5},{7,6},{8,9},{11,10},{12,13},{15,14},{17,16},{18,... | collective-permute-start | bytes 2654216 | tf_op jit(solution)/shard_map/ppermute | solution.py:32
  111.5 7.2 %collective-permute-start.11 = (s32[2,236]{1,0:T(2,128)S(1)}, s32[2,236]{1,0:T(2,128)S(1)}, u32[]{:S(2)}, u32[]{:S(2)}) collective-permute-start(s32[2,236]{1,0:T(2,128)S(1)} %fusion.22), channel_id=1, source_target_pairs={{0,16},{1,17},{2,18},{3,19},{4,20},{5,21},{6,22},{7,23},{8,24},{9,... | collective-permute-start | bytes 5672 | tf_op jit(solution)/shard_map/ppermute | solution.py:32
  125.7 8.2 %load_weights.1 = (bf16[768,2304]{1,0:T(8,128)(2,1)S(1)}, bf16[768,768]{1,0:T(8,128)(2,1)S(1)}, bf16[768,3072]{1,0:T(8,128)(2,1)S(1)}, bf16[768,3072]{1,0:T(8,12...) custom-call(s32[17]{0:T(128)S(1)} %stack.437.scal, ...), custom_call_target="tpu_custom_call" | custom-call | tf_op jit(solution)/shard_map/load_weights/pallas_call | solution.py:443
  133.9 8.2 %layer_forward.10 = (bf16[128,768]{1,0:T(8,128)(2,1)S(1)}, bf16[4,128,768]{2,1,0:T(8,128)(2,1)}, bf16[4,128,2304]{2,1,0:T(8,128)(2,1)}, f32[4,16,128]{2,1,0:T(8,...) custom-call(s32[4]{0:T(128)S(1)} %get-tuple-element.652.refs_0_, ...), custom_call_target="tpu_custom_call" | custom-call | flops 7516192768 | bytes 8388608 | tf_op jit(solution)/shard_map/layer_forward/pallas_call | solution.py:537
  145.8 6.2 %layer_forward.11 = (bf16[128,768]{1,0:T(8,128)(2,1)S(1)}, bf16[4,128,768]{2,1,0:T(8,128)(2,1)}, bf16[4,128,2304]{2,1,0:T(8,128)(2,1)}, f32[4,16,128]{2,1,0:T(8,...) custom-call(s32[4]{0:T(128)S(1)} %get-tuple-element.651.refs_0_, ...), custom_call_target="tpu_custom_call", output_to_operand_aliasing={{1}: (18, {}), {2}: (19, {}), {3}: (20, {}), {4}: (21, {}),... | custom-call | flops 7516192768 | bytes 8388608 | tf_op jit(solution)/shard_map/layer_forward/pallas_call | solution.py:537
  153.4 6.2 %layer_forward.12 = (bf16[128,768]{1,0:T(8,128)(2,1)S(1)}, bf16[4,128,768]{2,1,0:T(8,128)(2,1)}, bf16[4,128,2304]{2,1,0:T(8,128)(2,1)}, f32[4,16,128]{2,1,0:T(8,...) custom-call(s32[4]{0:T(128)S(1)} %add_add_fusion.6.refs_0_, ...), custom_call_target="tpu_custom_call", output_to_operand_aliasing={{1}: (18, {}), {2}: (19, {}), {3}: (20, {}), {4}: (21, {}),... | custom-call | flops 7516192768 | bytes 8388608 | tf_op jit(solution)/shard_map/layer_forward/pallas_call | solution.py:537
  160.9 7.8 %layer_forward.13 = (bf16[128,768]{1,0:T(8,128)(2,1)S(1)}, bf16[4,128,768]{2,1,0:T(8,128)(2,1)}, bf16[4,128,2304]{2,1,0:T(8,128)(2,1)}, f32[4,16,128]{2,1,0:T(8,...) custom-call(s32[4]{0:T(128)S(1)} %add_add_fusion.5.refs_0_, ...), custom_call_target="tpu_custom_call", output_to_operand_aliasing={{1}: (18, {}), {2}: (19, {}), {3}: (20, {}), {4}: (21, {}),... | custom-call | flops 7516192768 | bytes 8388608 | tf_op jit(solution)/shard_map/layer_forward/pallas_call | solution.py:537
  168.7 7.9 %collective-permute-start.26 = (bf16[128,768]{1,0:T(8,128)(2,1)S(1)}, bf16[128,768]{1,0:T(8,128)(2,1)S(1)}, u32[]{:S(2)}, u32[]{:S(2)}) collective-permute-start(bf16[128,768]{1,0:T(8,128)(2,1)S(1)} %get-tuple-element.411), channel_id=1, source_target_pairs={{0,16},{1,17},{4,20},{5,21},{8,24},{9,25},{12,28},{13,29},{16,18},... | collective-permute-start | bytes 589832 | tf_op jit(solution)/shard_map/ppermute | solution.py:32
  177.4 10.6 %collective-permute-start.29 = (bf16[128,768]{1,0:T(8,128)(2,1)S(1)}, bf16[128,768]{1,0:T(8,128)(2,1)S(1)}, u32[]{:S(2)}, u32[]{:S(2)}) collective-permute-start(bf16[128,768]{1,0:T(8,128)(2,1)S(1)} %get-tuple-element.440), channel_id=1, source_target_pairs={{0,16},{1,17},{4,20},{5,21},{8,24},{9,25},{12,28},{13,29},{16,18},... | collective-permute-start | bytes 589832 | tf_op jit(solution)/shard_map/ppermute | solution.py:32
  188.7 8.8 %collective-permute-start.28 = (bf16[128,768]{1,0:T(8,128)(2,1)S(1)}, bf16[128,768]{1,0:T(8,128)(2,1)S(1)}, u32[]{:S(2)}, u32[]{:S(2)}) collective-permute-start(bf16[128,768]{1,0:T(8,128)(2,1)S(1)} %get-tuple-element.439), channel_id=1, source_target_pairs={{0,16},{1,17},{4,20},{5,21},{8,24},{9,25},{12,28},{13,29},{16,18},... | collective-permute-start | bytes 589832 | tf_op jit(solution)/shard_map/ppermute | solution.py:32
  197.6 7.7 %layer_forward.16 = (bf16[128,768]{1,0:T(8,128)(2,1)S(1)}, bf16[4,128,768]{2,1,0:T(8,128)(2,1)}, bf16[4,128,2304]{2,1,0:T(8,128)(2,1)}, f32[4,16,128]{2,1,0:T(8,...) custom-call(s32[4]{0:T(128)S(1)} %add_add_fusion.8.refs_0_, ...), custom_call_target="tpu_custom_call", output_to_operand_aliasing={{1}: (18, {}), {2}: (19, {}), {3}: (20, {}), {4}: (21, {}),... | custom-call | flops 7516192768 | bytes 8388608 | tf_op jit(solution)/shard_map/layer_forward/pallas_call | solution.py:537
  215.3 9.3 %layer_forward.19 = (bf16[128,768]{1,0:T(8,128)(2,1)}, bf16[4,128,768]{2,1,0:T(8,128)(2,1)}, bf16[4,128,2304]{2,1,0:T(8,128)(2,1)}, f32[4,16,128]{2,1,0:T(8,128)...) custom-call(s32[4]{0:T(128)S(1)} %add_add_fusion.refs_0_, ...), custom_call_target="tpu_custom_call", output_to_operand_aliasing={{1}: (18, {}), {2}: (19, {}), {3}: (20, {}), {4}: (21, {}),... | custom-call | flops 7516192768 | bytes 8388608 | tf_op jit(solution)/shard_map/layer_forward/pallas_call | solution.py:537
  228.4 10.7 %collective-permute-done.33.refs_3_ = bf16[128,768]{1,0:T(8,128)(2,1)S(1)} collective-permute-done((bf16[128,768]{1,0:T(8,128)(2,1)S(1)}, bf16[128,768]{1,0:T(8,128)(2,1)S(1)}, u32[]{:S(2)}, u32[]{:S(2)}) %collective-permute-start.33) | collective-permute-done | bytes 196640 | tf_op jit(solution)/shard_map/ppermute | solution.py:32
  239.1 8.3 %layer_backward.12 = (bf16[128,768]{1,0:T(8,128)(2,1)S(1)}, bf16[4,128,768]{2,1,0:T(8,128)(2,1)S(1)}, bf16[4,128,3072]{2,1,0:T(8,128)(2,1)S(1)}, bf16[4,128,768]...) custom-call(s32[4]{0:T(128)S(1)} %add_add_fusion.16.refs_0_, ...), custom_call_target="tpu_custom_call", output_to_operand_aliasing={{1}: (15, {}), {2}: (16, {}), {3}: (17, {}), {4}: (18, {}),... | custom-call | flops 10737418240 | bytes 8388608 | tf_op jit(solution)/shard_map/layer_backward/pallas_call | solution.py:571
  258.7 8.8 %collective-permute-done.34.refs_3_ = bf16[128,768]{1,0:T(8,128)(2,1)S(1)} collective-permute-done((bf16[128,768]{1,0:T(8,128)(2,1)S(1)}, bf16[128,768]{1,0:T(8,128)(2,1)S(1)}, u32[]{:S(2)}, u32[]{:S(2)}) %collective-permute-start.34) | collective-permute-done | bytes 196640 | tf_op jit(solution)/shard_map/ppermute | solution.py:32
  267.5 8.5 %layer_backward.15 = (bf16[128,768]{1,0:T(8,128)(2,1)S(1)}, bf16[4,128,768]{2,1,0:T(8,128)(2,1)S(1)}, bf16[4,128,3072]{2,1,0:T(8,128)(2,1)S(1)}, bf16[4,128,768]...) custom-call(s32[4]{0:T(128)S(1)} %add_add_fusion.12.refs_0_, ...), custom_call_target="tpu_custom_call", output_to_operand_aliasing={{1}: (15, {}), {2}: (16, {}), {3}: (17, {}), {4}: (18, {}),... | custom-call | flops 10737418240 | bytes 8388608 | tf_op jit(solution)/shard_map/layer_backward/pallas_call | solution.py:571
  277.3 8.8 %collective-permute-done.37.refs_3_ = bf16[128,768]{1,0:T(8,128)(2,1)S(1)} collective-permute-done((bf16[128,768]{1,0:T(8,128)(2,1)S(1)}, bf16[128,768]{1,0:T(8,128)(2,1)S(1)}, u32[]{:S(2)}, u32[]{:S(2)}) %collective-permute-start.37) | collective-permute-done | bytes 196640 | tf_op jit(solution)/shard_map/ppermute | solution.py:32
  286.1 8.8 %layer_backward.16 = (bf16[128,768]{1,0:T(8,128)(2,1)S(1)}, bf16[4,128,768]{2,1,0:T(8,128)(2,1)S(1)}, bf16[4,128,3072]{2,1,0:T(8,128)(2,1)S(1)}, bf16[4,128,768]...) custom-call(s32[4]{0:T(128)S(1)} %add_add_fusion.18.refs_0_, ...), custom_call_target="tpu_custom_call", output_to_operand_aliasing={{1}: (15, {}), {2}: (16, {}), {3}: (17, {}), {4}: (18, {}),... | custom-call | flops 10737418240 | bytes 8388608 | tf_op jit(solution)/shard_map/layer_backward/pallas_call | solution.py:571
  297.1 8.8 %layer_backward.17 = (bf16[128,768]{1,0:T(8,128)(2,1)S(1)}, bf16[4,128,768]{2,1,0:T(8,128)(2,1)S(1)}, bf16[4,128,3072]{2,1,0:T(8,128)(2,1)S(1)}, bf16[4,128,768]...) custom-call(s32[4]{0:T(128)S(1)} %add_add_fusion.11.refs_0_, ...), custom_call_target="tpu_custom_call", output_to_operand_aliasing={{1}: (15, {}), {2}: (16, {}), {3}: (17, {}), {4}: (18, {}),... | custom-call | flops 10737418240 | bytes 8388608 | tf_op jit(solution)/shard_map/layer_backward/pallas_call | solution.py:571
  307.9 9.1 %layer_backward.18 = (bf16[128,768]{1,0:T(8,128)(2,1)S(1)}, bf16[4,128,768]{2,1,0:T(8,128)(2,1)S(1)}, bf16[4,128,3072]{2,1,0:T(8,128)(2,1)S(1)}, bf16[4,128,768]...) custom-call(s32[4]{0:T(128)S(1)} %add_add_fusion.19.refs_0_, ...), custom_call_target="tpu_custom_call", output_to_operand_aliasing={{1}: (15, {}), {2}: (16, {}), {3}: (17, {}), {4}: (18, {}),... | custom-call | flops 10737418240 | bytes 8388608 | tf_op jit(solution)/shard_map/layer_backward/pallas_call | solution.py:571
  318.7 9.3 %layer_backward.19 = (bf16[128,768]{1,0:T(8,128)(2,1)S(1)}, bf16[4,128,768]{2,1,0:T(8,128)(2,1)S(1)}, bf16[4,128,3072]{2,1,0:T(8,128)(2,1)S(1)}, bf16[4,128,768]...) custom-call(s32[4]{0:T(128)S(1)} %add_add_fusion.10.refs_0_, ...), custom_call_target="tpu_custom_call", output_to_operand_aliasing={{1}: (15, {}), {2}: (16, {}), {3}: (17, {}), {4}: (18, {}),... | custom-call | flops 10737418240 | bytes 8388608 | tf_op jit(solution)/shard_map/layer_backward/pallas_call | solution.py:571
  328.0 13.0 %weight_grads.1 = (bf16[3,96,3072]{2,1,0:T(8,128)(2,1)}, bf16[3,288,3072]{2,1,0:T(8,128)(2,1)}, bf16[3,384,3072]{2,1,0:T(8,128)(2,1)}) custom-call(s32[8]{0:T(128)S(1)} %stack.405.order, bf16[4,128,768]{2,1,0:T(8,128)(2,1)} %get-tuple-element.495.refs_0_, bf16[4,128,768]{2,1,0:T(8,128)(2,1)} %get-tuple-element.496.refs_1_, ...), custom_call_target="tpu_custom_call" | custom-call | flops 7247757312 | bytes 28311552 | tf_op jit(solution)/shard_map/weight_grads/pallas_call | solution.py:501
  354.4 19.4 %collective-permute-done.48 = bf16[128,768]{1,0:T(8,128)(2,1)S(1)} collective-permute-done((bf16[128,768]{1,0:T(8,128)(2,1)S(1)}, bf16[128,768]{1,0:T(8,128)(2,1)S(1)}, u32[]{:S(2)}, u32[]{:S(2)}) %collective-permute-start.48) | collective-permute-done | bytes 196640 | tf_op jit(solution)/shard_map/ppermute | solution.py:32
  393.3 9.5 %collective-permute-done.51 = f32[24,768]{1,0:T(8,128)S(1)} collective-permute-done((f32[24,768]{1,0:T(8,128)S(1)}, f32[24,768]{1,0:T(8,128)S(1)}, u32[]{:S(2)}, u32[]{:S(2)}) %collective-permute-start.51) | collective-permute-done | bytes 73760 | tf_op jit(solution)/shard_map/ppermute | solution.py:32
  403.6 5.5 %fusion.5 = bf16[3,96,3072]{2,1,0:T(8,128)(2,1)} fusion(bf16[3,96,3072]{2,1,0:T(8,128)(2,1)} %collective-permute-done.45, bf16[3,96,3072]{2,1,0:T(8,128)(2,1)} %collective-permute-done.44, bf16[3,4,96,3072]{3,2,1,0:T(8,128)(2,1)} %bitcast.220, bf16[3,3,96,3072]{3,2,1,0:T(8,128)(2,1)} %bitcast.88), kind=kLoop, calls=%fused_computation.11 | loop fusion | flops 7077888 | bytes 8847360 | tf_op jit(solution)/shard_map/convert_element_type | solution.py:803
  420.7 13.7 %collective-permute-done.54 = bf16[3,96,3072]{2,1,0:T(8,128)(2,1)} collective-permute-done((bf16[3,96,3072]{2,1,0:T(8,128)(2,1)}, bf16[3,96,3072]{2,1,0:T(8,128)(2,1)}, u32[]{:S(2)}, u32[]{:S(2)}) %collective-permute-start.54) | collective-permute-done | bytes 1769504 | tf_op jit(solution)/shard_map/ppermute | solution.py:32
  459.3 11.5 %collective-permute-start.61 = (f32[2,768]{1,0:T(2,128)S(1)}, f32[2,768]{1,0:T(2,128)S(1)}, u32[]{:S(2)}, u32[]{:S(2)}) collective-permute-start(f32[2,768]{1,0:T(2,128)S(1)} %slice.140), channel_id=1, source_target_pairs={{0,16},{1,17},{2,18},{3,19},{4,20},{5,21},{6,22},{7,23},{8,24},{9,... | collective-permute-start | bytes 18440 | tf_op jit(solution)/shard_map/ppermute | solution.py:32
  475.9 6.0 %collective-permute-done.60 = f32[20,768]{1,0:T(8,128)S(1)} collective-permute-done((f32[20,768]{1,0:T(8,128)S(1)}, f32[20,768]{1,0:T(8,128)S(1)}, u32[]{:S(2)}, u32[]{:S(2)}) %collective-permute-start.60) | collective-permute-done | bytes 61472 | tf_op jit(solution)/shard_map/ppermute | solution.py:32
  505.2 8.3 %multiply_subtract_fusion = (f32[1,3,96,3072]{3,2,1,0:T(8,128)}, f32[1,3,96,3072]{3,2,1,0:T(8,128)}, f32[1,3,96,3072]{3,2,1,0:T(8,128)}) fusion(f32[1,3,96,3072]{3,2,1,0:T(8,128)} %param.25, f32[]{:T(128)S(6)} %mul.468, bf16[3,96,3072]{2,1,0:T(8,128)(2,1)S(1)} %fusion.7, bf16[3,96,3072]{2,1,0:T(8,128)(2,1)} %collective-permute-done.53, pred[]{:T(512)S(6)} %eq.206, ...), kind=kLoop, calls=%fused_computation.14 | loop fusion | flops 15925248 | bytes 24772612 | tf_op jit(solution)/shard_map/sub | solution.py:614
  (322 shorter events, 212.8 us)
Async XLA Ops:
  4.4 31.1 %collective-permute-start = (bf16[2,3,48,3072]{3,2,1,0:T(8,128)(2,1)}, bf16[2,3,48,3072]{3,2,1,0:T(8,128)(2,1)}, u32[]{:S(2)}, u32[]{:S(2)}) collective-permute-start(bf16[2,3,48,3072]{3,2,1,0:T(8,128)(2,1)} %bitcast.213.refs_0_), channel_id=1, source_target_pairs={{1,16},{2,19},{5,20},{6,23},{9,24},{10,27},{13,28},{14,31},{16,1},... | collective-permute-start | bytes 5308424 | tf_op jit(solution)/shard_map/ppermute | solution.py:32
  6.5 29.0 %collective-permute-start.1 = (bf16[2,3,48,3072]{3,2,1,0:T(8,128)(2,1)}, bf16[2,3,48,3072]{3,2,1,0:T(8,128)(2,1)}, u32[]{:S(2)}, u32[]{:S(2)}) collective-permute-start(bf16[2,3,48,3072]{3,2,1,0:T(8,128)(2,1)} %bitcast.213.refs_0_), channel_id=1, source_target_pairs={{0,4},{3,7},{4,0},{7,3},{8,12},{11,15},{12,8},{15,11},{17,21},{18,... | collective-permute-start | bytes 5308424 | tf_op jit(solution)/shard_map/ppermute | solution.py:32
  11.3 42.6 %collective-permute-start.2 = (bf16[2,3,48,3072]{3,2,1,0:T(8,128)(2,1)}, bf16[2,3,48,3072]{3,2,1,0:T(8,128)(2,1)}, u32[]{:S(2)}, u32[]{:S(2)}) collective-permute-start(bf16[2,3,48,3072]{3,2,1,0:T(8,128)(2,1)} %bitcast.213.refs_0_), channel_id=1, source_target_pairs={{0,8},{3,11},{4,12},{7,15},{8,0},{11,3},{12,4},{15,7},{17,25},{18,... | collective-permute-start | bytes 5308424 | tf_op jit(solution)/shard_map/ppermute | solution.py:32
  14.8 50.5 %collective-permute-start.7 = (bf16[2,3,48,3072]{3,2,1,0:T(8,128)(2,1)}, bf16[2,3,48,3072]{3,2,1,0:T(8,128)(2,1)}, u32[]{:S(2)}, u32[]{:S(2)}) collective-permute-start(bf16[2,3,48,3072]{3,2,1,0:T(8,128)(2,1)} %bitcast.213.refs_0_), channel_id=1, source_target_pairs={{0,1},{3,2},{4,5},{7,6},{8,9},{11,10},{12,13},{15,14},{17,16},{18,... | collective-permute-start | bytes 5308424 | tf_op jit(solution)/shard_map/ppermute | solution.py:32
  34.3 29.0 %collective-permute-start.10 = (bf16[2,1,416,768]{3,2,1,0:T(8,128)(2,1)S(1)}, bf16[2,1,416,768]{3,2,1,0:T(8,128)(2,1)S(1)}, u32[]{:S(2)}, u32[]{:S(2)}) collective-permute-start(bf16[2,1,416,768]{3,2,1,0:T(8,128)(2,1)S(1)} %pad_maximum_fusion), channel_id=1, source_target_pairs={{0,1},{1,0},{2,3},{3,2},{4,5},{5,4},{6,7},{7,6},{8,9},{9,8},{10,11... | collective-permute-start | bytes 3833864 | tf_op jit(solution)/shard_map/ppermute | solution.py:32
  53.9 34.4 %collective-permute-start.3 = (bf16[2,3,48,3072]{3,2,1,0:T(8,128)(2,1)}, bf16[2,3,48,3072]{3,2,1,0:T(8,128)(2,1)}, u32[]{:S(2)}, u32[]{:S(2)}) collective-permute-start(bf16[2,3,48,3072]{3,2,1,0:T(8,128)(2,1)} %collective-permute-done.refs_10_), channel_id=1, source_target_pairs={{1,5},{2,6},{5,1},{6,2},{9,13},{10,14},{13,9},{14,10},{16,20},{19,... | collective-permute-start | bytes 5308424 | tf_op jit(solution)/shard_map/ppermute | solution.py:32
  55.8 32.6 %collective-permute-start.4 = (bf16[2,3,48,3072]{3,2,1,0:T(8,128)(2,1)}, bf16[2,3,48,3072]{3,2,1,0:T(8,128)(2,1)}, u32[]{:S(2)}, u32[]{:S(2)}) collective-permute-start(bf16[2,3,48,3072]{3,2,1,0:T(8,128)(2,1)} %collective-permute-done.refs_10_), channel_id=1, source_target_pairs={{1,9},{2,10},{5,13},{6,14},{9,1},{10,2},{13,5},{14,6},{16,24},{19,... | collective-permute-start | bytes 5308424 | tf_op jit(solution)/shard_map/ppermute | solution.py:32
  57.7 30.7 %collective-permute-start.8 = (bf16[2,3,48,3072]{3,2,1,0:T(8,128)(2,1)}, bf16[2,3,48,3072]{3,2,1,0:T(8,128)(2,1)}, u32[]{:S(2)}, u32[]{:S(2)}) collective-permute-start(bf16[2,3,48,3072]{3,2,1,0:T(8,128)(2,1)} %collective-permute-done.refs_10_), channel_id=1, source_target_pairs={{1,0},{2,3},{5,4},{6,7},{9,8},{10,11},{13,12},{14,15},{16,17},{19,... | collective-permute-start | bytes 5308424 | tf_op jit(solution)/shard_map/ppermute | solution.py:32
  63.2 20.1 %collective-permute-start.5 = (bf16[3,48,3072]{2,1,0:T(8,128)(2,1)}, bf16[3,48,3072]{2,1,0:T(8,128)(2,1)}, u32[]{:S(2)}, u32[]{:S(2)}) collective-permute-start(bf16[3,48,3072]{2,1,0:T(8,128)(2,1)} %slice_bitcast_fusion.11), channel_id=1, source_target_pairs={{0,4},{3,7},{4,0},{7,3},{8,12},{11,15},{12,8},{15,11},{17,21},{18,... | collective-permute-start | bytes 2654216 | tf_op jit(solution)/shard_map/ppermute | solution.py:32
  65.3 21.2 %collective-permute-start.6 = (bf16[3,48,3072]{2,1,0:T(8,128)(2,1)}, bf16[3,48,3072]{2,1,0:T(8,128)(2,1)}, u32[]{:S(2)}, u32[]{:S(2)}) collective-permute-start(bf16[3,48,3072]{2,1,0:T(8,128)(2,1)} %slice_bitcast_fusion.10), channel_id=1, source_target_pairs={{0,8},{3,11},{4,12},{7,15},{8,0},{11,3},{12,4},{15,7},{17,25},{18,... | collective-permute-start | bytes 2654216 | tf_op jit(solution)/shard_map/ppermute | solution.py:32
  89.6 29.1 %collective-permute-start.20 = (bf16[2,3,48,3072]{3,2,1,0:T(8,128)(2,1)}, bf16[2,3,48,3072]{3,2,1,0:T(8,128)(2,1)}, u32[]{:S(2)}, u32[]{:S(2)}) collective-permute-start(bf16[2,3,48,3072]{3,2,1,0:T(8,128)(2,1)} %collective-permute-done.4.refs_12_), channel_id=1, source_target_pairs={{1,0},{2,3},{5,4},{6,7},{9,8},{10,11},{13,12},{14,15},{16,17},{19,... | collective-permute-start | bytes 5308424 | tf_op jit(solution)/shard_map/ppermute | solution.py:32
  91.7 27.1 %collective-permute-start.19 = (bf16[2,3,48,3072]{3,2,1,0:T(8,128)(2,1)}, bf16[2,3,48,3072]{3,2,1,0:T(8,128)(2,1)}, u32[]{:S(2)}, u32[]{:S(2)}) collective-permute-start(bf16[2,3,48,3072]{3,2,1,0:T(8,128)(2,1)} %collective-permute-done.3.refs_11_), channel_id=1, source_target_pairs={{1,0},{2,3},{5,4},{6,7},{9,8},{10,11},{13,12},{14,15},{16,17},{19,... | collective-permute-start | bytes 5308424 | tf_op jit(solution)/shard_map/ppermute | solution.py:32
  96.8 22.0 %collective-permute-start.17 = (bf16[3,48,3072]{2,1,0:T(8,128)(2,1)}, bf16[3,48,3072]{2,1,0:T(8,128)(2,1)}, u32[]{:S(2)}, u32[]{:S(2)}) collective-permute-start(bf16[3,48,3072]{2,1,0:T(8,128)(2,1)} %collective-permute-done.5.refs_3_), channel_id=1, source_target_pairs={{0,1},{3,2},{4,5},{7,6},{8,9},{11,10},{12,13},{15,14},{17,16},{18,... | collective-permute-start | bytes 2654216 | tf_op jit(solution)/shard_map/ppermute | solution.py:32
  122.6 30.7 %collective-permute-start.23 = (bf16[2,128,768]{2,1,0:T(8,128)(2,1)S(1)}, bf16[2,128,768]{2,1,0:T(8,128)(2,1)S(1)}, u32[]{:S(2)}, u32[]{:S(2)}) collective-permute-start(bf16[2,128,768]{2,1,0:T(8,128)(2,1)S(1)} %constant_dynamic-slice_fusion.3), channel_id=1, source_target_pairs={{16,0},{17,1},{20,4},{21,5},{24,8},{25,9},{28,12},{29,13}} | collective-permute-start | bytes 1179656 | tf_op jit(solution)/shard_map/ppermute | solution.py:32
  159.6 17.0 %collective-permute-start.27 = (bf16[128,768]{1,0:T(8,128)(2,1)S(1)}, bf16[128,768]{1,0:T(8,128)(2,1)S(1)}, u32[]{:S(2)}, u32[]{:S(2)}) collective-permute-start(bf16[128,768]{1,0:T(8,128)(2,1)S(1)} %get-tuple-element.412), channel_id=1, source_target_pairs={{0,16},{1,17},{4,20},{5,21},{8,24},{9,25},{12,28},{13,29},{16,18},... | collective-permute-start | bytes 589832 | tf_op jit(solution)/shard_map/ppermute | solution.py:32
  168.7 19.3 %collective-permute-start.26 = (bf16[128,768]{1,0:T(8,128)(2,1)S(1)}, bf16[128,768]{1,0:T(8,128)(2,1)S(1)}, u32[]{:S(2)}, u32[]{:S(2)}) collective-permute-start(bf16[128,768]{1,0:T(8,128)(2,1)S(1)} %get-tuple-element.411), channel_id=1, source_target_pairs={{0,16},{1,17},{4,20},{5,21},{8,24},{9,25},{12,28},{13,29},{16,18},... | collective-permute-start | bytes 589832 | tf_op jit(solution)/shard_map/ppermute | solution.py:32
  177.4 20.2 %collective-permute-start.29 = (bf16[128,768]{1,0:T(8,128)(2,1)S(1)}, bf16[128,768]{1,0:T(8,128)(2,1)S(1)}, u32[]{:S(2)}, u32[]{:S(2)}) collective-permute-start(bf16[128,768]{1,0:T(8,128)(2,1)S(1)} %get-tuple-element.440), channel_id=1, source_target_pairs={{0,16},{1,17},{4,20},{5,21},{8,24},{9,25},{12,28},{13,29},{16,18},... | collective-permute-start | bytes 589832 | tf_op jit(solution)/shard_map/ppermute | solution.py:32
  188.7 18.4 %collective-permute-start.28 = (bf16[128,768]{1,0:T(8,128)(2,1)S(1)}, bf16[128,768]{1,0:T(8,128)(2,1)S(1)}, u32[]{:S(2)}, u32[]{:S(2)}) collective-permute-start(bf16[128,768]{1,0:T(8,128)(2,1)S(1)} %get-tuple-element.439), channel_id=1, source_target_pairs={{0,16},{1,17},{4,20},{5,21},{8,24},{9,25},{12,28},{13,29},{16,18},... | collective-permute-start | bytes 589832 | tf_op jit(solution)/shard_map/ppermute | solution.py:32
  227.1 22.9 %collective-permute-start.32 = (bf16[128,768]{1,0:T(8,128)(2,1)S(1)}, bf16[128,768]{1,0:T(8,128)(2,1)S(1)}, u32[]{:S(2)}, u32[]{:S(2)}) collective-permute-start(bf16[128,768]{1,0:T(8,128)(2,1)S(1)} %get-tuple-element.509), channel_id=1, source_target_pairs={{2,18},{3,19},{6,22},{7,23},{10,26},{11,27},{14,30},{15,31},{16,0}... | collective-permute-start | bytes 589832 | tf_op jit(solution)/shard_map/ppermute | solution.py:32
  257.4 28.7 %collective-permute-start.37 = (bf16[128,768]{1,0:T(8,128)(2,1)S(1)}, bf16[128,768]{1,0:T(8,128)(2,1)S(1)}, u32[]{:S(2)}, u32[]{:S(2)}) collective-permute-start(bf16[128,768]{1,0:T(8,128)(2,1)S(1)} %get-tuple-element.534), channel_id=1, source_target_pairs={{2,18},{3,19},{6,22},{7,23},{10,26},{11,27},{14,30},{15,31},{16,0}... | collective-permute-start | bytes 589832 | tf_op jit(solution)/shard_map/ppermute | solution.py:32
  276.0 21.1 %collective-permute-start.36 = (bf16[128,768]{1,0:T(8,128)(2,1)S(1)}, bf16[128,768]{1,0:T(8,128)(2,1)S(1)}, u32[]{:S(2)}, u32[]{:S(2)}) collective-permute-start(bf16[128,768]{1,0:T(8,128)(2,1)S(1)} %get-tuple-element.533), channel_id=1, source_target_pairs={{2,18},{3,19},{6,22},{7,23},{10,26},{11,27},{14,30},{15,31},{16,0}... | collective-permute-start | bytes 589832 | tf_op jit(solution)/shard_map/ppermute | solution.py:32
  344.9 33.9 %collective-permute-start.41 = (bf16[3,288,3072]{2,1,0:T(8,128)(2,1)}, bf16[3,288,3072]{2,1,0:T(8,128)(2,1)}, u32[]{:S(2)}, u32[]{:S(2)}) collective-permute-start(bf16[3,288,3072]{2,1,0:T(8,128)(2,1)} %get-tuple-element.565), channel_id=1, source_target_pairs={{0,1},{1,0},{2,3},{3,2},{4,5},{5,4},{6,7},{7,6},{8,9},{9,8},{10,11... | collective-permute-start | bytes 15925256 | tf_op jit(solution)/shard_map/ppermute | solution.py:32
  348.4 30.4 %collective-permute-start.42 = (bf16[3,48,3072]{2,1,0:T(8,128)(2,1)}, bf16[3,48,3072]{2,1,0:T(8,128)(2,1)}, u32[]{:S(2)}, u32[]{:S(2)}) collective-permute-start(bf16[3,48,3072]{2,1,0:T(8,128)(2,1)} %get-tuple-element.566), channel_id=1, source_target_pairs={{0,4},{1,5},{2,6},{3,7},{4,0},{5,1},{6,2},{7,3},{8,12},{9,13},{10,... | collective-permute-start | bytes 2654216 | tf_op jit(solution)/shard_map/ppermute | solution.py:32
  349.3 29.5 %collective-permute-start.43 = (bf16[3,48,3072]{2,1,0:T(8,128)(2,1)}, bf16[3,48,3072]{2,1,0:T(8,128)(2,1)}, u32[]{:S(2)}, u32[]{:S(2)}) collective-permute-start(bf16[3,48,3072]{2,1,0:T(8,128)(2,1)} %get-tuple-element.567), channel_id=1, source_target_pairs={{0,8},{1,9},{2,10},{3,11},{4,12},{5,13},{6,14},{7,15},{8,0},{9,1},... | collective-permute-start | bytes 2654216 | tf_op jit(solution)/shard_map/ppermute | solution.py:32
  349.3 24.4 %collective-permute-start.48 = (bf16[128,768]{1,0:T(8,128)(2,1)S(1)}, bf16[128,768]{1,0:T(8,128)(2,1)S(1)}, u32[]{:S(2)}, u32[]{:S(2)}) collective-permute-start(bf16[128,768]{1,0:T(8,128)(2,1)S(1)} %get-tuple-element.575), channel_id=1, source_target_pairs={{0,16},{1,17},{4,20},{5,21},{8,24},{9,25},{12,28},{13,29}} | collective-permute-start | bytes 589832 | tf_op jit(solution)/shard_map/ppermute | solution.py:32
  351.7 25.7 %collective-permute-start.47 = (bf16[128,768]{1,0:T(8,128)(2,1)S(1)}, bf16[128,768]{1,0:T(8,128)(2,1)S(1)}, u32[]{:S(2)}, u32[]{:S(2)}) collective-permute-start(bf16[128,768]{1,0:T(8,128)(2,1)S(1)} %get-tuple-element.580), channel_id=1, source_target_pairs={{0,16},{1,17},{4,20},{5,21},{8,24},{9,25},{12,28},{13,29}} | collective-permute-start | bytes 589832 | tf_op jit(solution)/shard_map/ppermute | solution.py:32
  384.2 19.4 %collective-permute-start.44 = (bf16[3,96,3072]{2,1,0:T(8,128)(2,1)}, bf16[3,96,3072]{2,1,0:T(8,128)(2,1)}, u32[]{:S(2)}, u32[]{:S(2)}) collective-permute-start(bf16[3,96,3072]{2,1,0:T(8,128)(2,1)} %get-tuple-element.586), channel_id=1, source_target_pairs={{1,5},{2,6},{5,1},{6,2},{9,13},{10,14},{13,9},{14,10},{16,20},{19,... | collective-permute-start | bytes 5308424 | tf_op jit(solution)/shard_map/ppermute | solution.py:32
  386.1 17.5 %collective-permute-start.45 = (bf16[3,96,3072]{2,1,0:T(8,128)(2,1)}, bf16[3,96,3072]{2,1,0:T(8,128)(2,1)}, u32[]{:S(2)}, u32[]{:S(2)}) collective-permute-start(bf16[3,96,3072]{2,1,0:T(8,128)(2,1)} %get-tuple-element.587), channel_id=1, source_target_pairs={{1,9},{2,10},{5,13},{6,14},{9,1},{10,2},{13,5},{14,6},{16,24},{19,... | collective-permute-start | bytes 5308424 | tf_op jit(solution)/shard_map/ppermute | solution.py:32
  409.1 25.3 %collective-permute-start.54 = (bf16[3,96,3072]{2,1,0:T(8,128)(2,1)}, bf16[3,96,3072]{2,1,0:T(8,128)(2,1)}, u32[]{:S(2)}, u32[]{:S(2)}) collective-permute-start(bf16[3,96,3072]{2,1,0:T(8,128)(2,1)} %get-tuple-element.586), channel_id=1, source_target_pairs={{0,4},{3,7},{4,0},{7,3},{8,12},{11,15},{12,8},{15,11},{17,21},{18,... | collective-permute-start | bytes 5308424 | tf_op jit(solution)/shard_map/ppermute | solution.py:32
  412.0 25.1 %collective-permute-start.55 = (bf16[3,96,3072]{2,1,0:T(8,128)(2,1)}, bf16[3,96,3072]{2,1,0:T(8,128)(2,1)}, u32[]{:S(2)}, u32[]{:S(2)}) collective-permute-start(bf16[3,96,3072]{2,1,0:T(8,128)(2,1)} %get-tuple-element.587), channel_id=1, source_target_pairs={{0,8},{3,11},{4,12},{7,15},{8,0},{11,3},{12,4},{15,7},{17,25},{18,... | collective-permute-start | bytes 5308424 | tf_op jit(solution)/shard_map/ppermute | solution.py:32
  415.7 69.2 %collective-permute-start.53 = (bf16[3,96,3072]{2,1,0:T(8,128)(2,1)}, bf16[3,96,3072]{2,1,0:T(8,128)(2,1)}, u32[]{:S(2)}, u32[]{:S(2)}) collective-permute-start(bf16[3,96,3072]{2,1,0:T(8,128)(2,1)} %fusion.5), channel_id=1, source_target_pairs={{1,16},{2,19},{5,20},{6,23},{9,24},{10,27},{13,28},{14,31},{16,1},... | collective-permute-start | bytes 5308424 | tf_op jit(solution)/shard_map/ppermute | solution.py:32
  454.6 18.2 %collective-permute-start.59 = (f32[20,768]{1,0:T(8,128)}, f32[20,768]{1,0:T(8,128)S(1)}, u32[]{:S(2)}, u32[]{:S(2)}) collective-permute-start(f32[20,768]{1,0:T(8,128)} %slice_select_fusion.1), channel_id=1, source_target_pairs={{0,2},{1,3},{2,0},{3,1},{4,6},{5,7},{6,4},{7,5},{8,10},{9,11},{10,... | collective-permute-start | bytes 184328 | tf_op jit(solution)/shard_map/ppermute | solution.py:32
  (71 other events, 978.2 us)
